TPU v7x, 32 devices: a whole 2x2x4 slice. The times are simulated.
32 devices in a mesh: row: 2 (over x), col: 8 (over z, core), dp: 2 (over y).
Axes of the slice: x: 2, y: 2, z: 4, core: 2. Of those that a mesh axis runs over, the one named last changes fastest.
Arguments:
- layer_input: bfloat16 [512, 12288], P(('dp', 'col'), 'row'), parts along dimension 0, may hold values from -6 to 6
- layer_norm_gain: float32 [12288], P('row'), may hold values from 0.1 to 1.9
- w_qkv: bfloat16 [12288, 18432], P('row', 'col'), may hold values from -16 to 16
- w_out: bfloat16 [6144, 12288], P('col', 'row'), may hold values from -0.078125 to 0.078125
- out_grad: bfloat16 [512, 12288], P(('dp', 'col'), 'row'), parts along dimension 0, may hold values from -6 to 6
Outputs:
- input_gradient: bfloat16 [512, 12288], P(('dp', 'col'), 'row'), parts along dimension 0
- gain_gradient: float32 [24576], P(('dp', 'row')), parts along dimension 0
- grad_wqkv: bfloat16 [24576, 18432], P(('dp', 'row'), 'col'), parts along dimension 0
- grad_wout: bfloat16 [12288, 12288], P(('dp', 'col'), 'row'), parts along dimension 0
There are 2 independent parts, one for each index of `dp`. A program takes and returns all parts, laid end to end along the dimension named above; an argument that names none is the same for every part. Nothing has to cross between parts.
All inputs are finite; a program needn't handle non-finite values.
Results may differ from a plain program's by a relative error of at most 0.0098.
Values may be sent and summed in bfloat16 or wider, within the bound.
A program may use at most 128 MiB of HBM per device.

v0:
```python
import math

import jax
import jax.numpy as jnp
from jax import lax
from jax.sharding import PartitionSpec as P

HS = 128


EPS = 1e-05


def shards(layer_input, layer_norm_gain, w_qkv, w_out, out_grad):
    rows_here, features_here = layer_input.shape
    col_count = lax.axis_size("col")
    row_count = lax.axis_size("row")
    tokens = rows_here * col_count
    tok_row = tokens // row_count
    feature_width = features_here * row_count
    heads_here = w_qkv.shape[1] // (3 * HS)
    scale = 1.0 / math.sqrt(HS)
    input_float = layer_input.astype(jnp.float32)
    average = lax.psum(jnp.sum(input_float, axis=1), "row") / feature_width
    centered_input = input_float - average[:, None]
    variance = lax.psum(jnp.sum(centered_input * centered_input, axis=1), "row") / feature_width
    inverse_deviation = lax.rsqrt(variance + EPS)
    standardized_input = centered_input * inverse_deviation[:, None]
    normalized_output = (standardized_input * layer_norm_gain[None, :]).astype(jnp.bfloat16)
    normed_all = lax.all_gather(normalized_output, "col", axis=0, tiled=True)
    first_query = lax.axis_index("row") * tok_row
    piece = normed_all
    owned = lax.psum_scatter(
        jnp.dot(piece, w_qkv, preferred_element_type=jnp.float32),
        "row",
        scatter_dimension=0,
        tiled=True,
    ).astype(jnp.bfloat16)
    owned = owned.reshape(tok_row, heads_here, 3, HS)
    query = owned[:, :, 0]
    key_value = lax.all_gather(owned[:, :, 1:], "row", axis=0, tiled=True)
    keys = key_value[:, :, 0]
    values = key_value[:, :, 1]
    query_pos = first_query + jnp.arange(tok_row)
    key_pos = jnp.arange(tokens)
    allowed = key_pos[None, :] <= query_pos[:, None]
    scores = jnp.einsum("qhe,khe->hqk", query, keys, preferred_element_type=jnp.float32) * scale
    scores = jnp.where(allowed[None], scores, -jnp.inf)
    highest = jnp.max(scores, axis=2, keepdims=True)
    powers = jnp.exp(scores - highest)
    totals = jnp.sum(powers, axis=2, keepdims=True)
    probs = powers / totals
    probs_b = probs.astype(jnp.bfloat16)
    context = jnp.einsum(
        "hqk,khe->qhe", probs_b, values, preferred_element_type=jnp.float32
    ).astype(jnp.bfloat16)
    context_all = lax.all_gather(
        context.reshape(tok_row, heads_here * HS), "row", axis=0, tiled=True
    )
    grad_all = lax.all_gather(out_grad, "col", axis=0, tiled=True)
    grad_wout = lax.dot_general(
        context_all, grad_all, (((0,), (0,)), ((), ())), preferred_element_type=jnp.float32
    ).astype(jnp.bfloat16)
    piece = grad_all
    d_context = lax.psum_scatter(
        lax.dot_general(piece, w_out, (((1,), (1,)), ((), ())), preferred_element_type=jnp.float32),
        "row",
        scatter_dimension=0,
        tiled=True,
    ).astype(jnp.bfloat16)
    d_context = d_context.reshape(tok_row, heads_here, HS)
    d_probs = jnp.einsum("qhe,khe->hqk", d_context, values, preferred_element_type=jnp.float32)
    delta = jnp.sum(probs * d_probs, axis=2, keepdims=True)
    d_scores = (probs * (d_probs - delta) * scale).astype(jnp.bfloat16)
    d_query = jnp.einsum("hqk,khe->qhe", d_scores, keys, preferred_element_type=jnp.float32).astype(
        jnp.bfloat16
    )
    d_keys = jnp.einsum("hqk,qhe->khe", d_scores, query, preferred_element_type=jnp.float32)
    d_values = jnp.einsum("hqk,qhe->khe", probs_b, d_context, preferred_element_type=jnp.float32)
    d_pairs = jnp.stack([d_keys, d_values], axis=2)
    pair_owned = lax.psum_scatter(d_pairs, "row", scatter_dimension=0, tiled=True).astype(
        jnp.bfloat16
    )
    owned_grad = jnp.concatenate([d_query[:, :, None], pair_owned], axis=2)
    owned_grad = owned_grad.reshape(tok_row, heads_here * 3 * HS)
    d_qkv_all = lax.all_gather(owned_grad, "row", axis=0, tiled=True)
    grad_wqkv = lax.dot_general(
        normed_all, d_qkv_all, (((0,), (0,)), ((), ())), preferred_element_type=jnp.float32
    ).astype(jnp.bfloat16)
    piece = d_qkv_all
    normalized_gradient = lax.psum_scatter(
        lax.dot_general(piece, w_qkv, (((1,), (1,)), ((), ())), preferred_element_type=jnp.float32),
        "col",
        scatter_dimension=0,
        tiled=True,
    )
    gain_gradient = lax.psum(jnp.sum(normalized_gradient * standardized_input, axis=0), "col")
    scaled_gradient = normalized_gradient * layer_norm_gain[None, :]
    first_term_sum, second_term_sum = lax.psum(
        (jnp.sum(scaled_gradient, axis=1), jnp.sum(scaled_gradient * standardized_input, axis=1)),
        "row",
    )
    input_gradient = inverse_deviation[:, None] * (
        scaled_gradient
        - first_term_sum[:, None] / feature_width
        - standardized_input * (second_term_sum[:, None] / feature_width)
    )
    return (input_gradient.astype(jnp.bfloat16), gain_gradient, grad_wqkv, grad_wout)


def solution(mesh):
    in_specs = (
        P(("dp", "col"), "row"),
        P("row"),
        P("row", "col"),
        P("col", "row"),
        P(("dp", "col"), "row"),
    )
    out_specs = (
        P(("dp", "col"), "row"),
        P(("dp", "row")),
        P(("dp", "row"), "col"),
        P(("dp", "col"), "row"),
    )
    return jax.shard_map(shards, mesh=mesh, in_specs=in_specs, out_specs=out_specs, check_vma=False)
```

profile of v0, /device:TPU:0, one launch (start us, length us, event | category | flops | bytes accessed | tf_op | source)
XLA Modules:
  0.0 351.2 jit_solution(4287343713329217369)
XLA Ops:
  7.2 0.0 all-gather.6.cloned.1.call-start
  7.2 0.7 all-gather.6.cloned.1.call-update
  7.9 0.0 all-gather.4.cloned.1.call-start
  7.9 1.2 convert_reduce_fusion
  9.1 5.8 %psum.35 = f32[32]{0:T(128)S(1)} all-reduce(f32[32]{0:T(128)S(1)} %convert_reduce_fusion), channel_id=1, replica_groups=mesh['row'=2,'col'=8,'dp'=2] {'row'}, use_global_device_ids=true, to_apply=%region_1.0 | all-reduce | flops 32 | bytes 256 | tf_op jit(solution)/shard_map/psum | solution.py:24
  14.9 1.3 fusion.22
  16.2 4.9 %psum.36 = f32[32]{0:T(128)S(1)} all-reduce(f32[32]{0:T(128)S(1)} %fusion.22), channel_id=1, replica_groups=mesh['row'=2,'col'=8,'dp'=2] {'row'}, use_global_device_ids=true, to_apply=%region_3.0 | all-reduce | flops 32 | bytes 256 | tf_op jit(solution)/shard_map/psum | solution.py:26
  21.2 1.9 fusion.16
  23.1 0.0 all-gather.4.cloned.1.call-update
  23.1 0.0 reduce-scatter.7.cloned.1.call-start
  23.2 27.5 %all-gather.6.cloned.1.call-done = bf16[256,6144]{1,0:T(8,128)(2,1)} async-done(((bf16[32,6144]{1,0:T(8,128)(2,1)}), bf16[256,6144]{1,0:T(8,128)(2,1)}) %all-gather.6.cloned.1.call-update) | async-done | bytes 3145744 | tf_op jit(solution)/shard_map/all_gather | solution.py:60
  50.7 8.2 %fusion.42 = f32[256,768]{1,0:T(8,128)} fusion(bf16[256,6144]{1,0:T(8,128)(2,1)} %all-gather.6.cloned.1.call-done, bf16[768,6144]{1,0:T(8,128)(2,1)} %param.8), kind=kOutput, calls=%fused_computation.61 | convolution fusion | flops 2415919104 | bytes 13369344 | tf_op jit(solution)/shard_map/dot_general | solution.py:66
  58.8 0.0 reduce-scatter.7.cloned.1.call-update
  58.8 0.0 reduce-scatter.5.cloned.1.call-start
  58.9 31.2 %all-gather.4.cloned.1.call-done = bf16[256,6144]{1,0:T(8,128)(2,1)} async-done(((bf16[32,6144]{1,0:T(8,128)(2,1)}), bf16[256,6144]{1,0:T(8,128)(2,1)}) %all-gather.4.cloned.1.call-update) | async-done | bytes 3145744 | tf_op jit(solution)/shard_map/all_gather | solution.py:30
  90.1 15.5 %fusion.41 = f32[256,2304]{1,0:T(8,128)} fusion(bf16[256,6144]{1,0:T(8,128)(2,1)} %all-gather.4.cloned.1.call-done, bf16[6144,2304]{1,0:T(8,128)(2,1)} %param.7), kind=kOutput, calls=%fused_computation.60 | convolution fusion | flops 7247757312 | bytes 33816576 | tf_op jit(solution)/shard_map/dot_general | solution.py:34
  105.5 0.0 reduce-scatter.5.cloned.1.call-update
  105.5 0.0 reduce-scatter.9.cloned.1.call-start
  105.6 0.1 iota_compare_fusion
  105.7 3.5 reduce-scatter.7.cloned.1.call-done
  109.2 1.0 convert_element_type.45
  110.2 0.2 copy.19
  110.4 36.3 %reduce-scatter.5.cloned.1.call-done = f32[128,2304]{1,0:T(8,128)} async-done(((f32[256,2304]{1,0:T(8,128)}), f32[128,2304]{1,0:T(8,128)}) %reduce-scatter.5.cloned.1.call-update) | async-done | bytes 1179664 | tf_op jit(solution)/shard_map/reduce_scatter | solution.py:33
  146.7 1.3 convert_element_type.44
  148.1 0.3 copy.16
  148.4 0.2 copy.29
  148.6 11.5 %all_gather.16 = bf16[256,6,2,128]{3,0,1,2:T(8,128)(2,1)S(1)} all-gather(bf16[128,6,2,128]{3,0,1,2:T(8,128)(2,1)S(1)} %copy.29), channel_id=1, replica_groups=mesh['row'=2,'col'=8,'dp'=2] {'row'}, dimensions={0}, use_global_device_ids=true | all-gather | bytes 1179648 | tf_op jit(solution)/shard_map/all_gather | solution.py:41
  160.2 1.3 fusion.40
  161.5 0.3 fusion.30
  161.8 1.5 convolution_bitcast_fusion
  163.3 6.3 %convolution_bitcast_fusion.1 = f32[256,6,1,128]{0,3,1,2:T(8,128)} fusion(f32[6,128,256]{2,1,0:T(8,128)S(1)} %fusion.30, bf16[128,6,3,128]{0,3,2,1:T(8,128)(2,1)S(1)} %bitcast.59, f32[6,128,256]{2,1,0:T(8,128)} %get-tuple-element.10, f32[6,128]{1,0:T(8,128)S(1)} %get-tuple-element.9), kind=kOutput, calls=%fused_computation.11 | convolution fusion | flops 51708928 | bytes 4136960 | tf_op jit(solution)/shard_map/hqk,qhe->khe/dot_general | solution.py:78
  169.6 2.4 pad_maximum_fusion
  172.0 0.0 reduce-scatter.9.cloned.1.call-update
  172.0 0.0 all-gather.8.cloned.1.call-start
  172.1 6.0 %fusion.9 = bf16[128,6,1,128]{0,3,1,2:T(8,128)(2,1)S(1)} fusion(f32[6,128,256]{2,1,0:T(8,128)S(1)} %fusion.30, bf16[256,6,2,128]{3,0,1,2:T(8,128)(2,1)S(1)} %all_gather.16, f32[6,128,256]{2,1,0:T(8,128)} %get-tuple-element.10, f32[6,128]{1,0:T(8,128)S(1)} %get-tuple-element.9), kind=kOutput, calls=%fused_computation.17 | convolution fusion | flops 51807232 | bytes 3743744 | tf_op jit(solution)/shard_map/hqk,khe->qhe/dot_general | solution.py:75
  178.0 20.2 %reduce-scatter.9.cloned.1.call-done = f32[128,6,2,128]{0,3,1,2:T(8,128)} async-done(((f32[256,6,2,128]{0,3,1,2:T(8,128)}), f32[128,6,2,128]{0,3,1,2:T(8,128)}) %reduce-scatter.9.cloned.1.call-update) | async-done | bytes 786448 | tf_op jit(solution)/shard_map/reduce_scatter | solution.py:81
  198.3 1.2 convert_element_type.50
  199.5 0.1 pad_maximum_fusion.1
  199.5 0.9 copy.23
  200.4 0.0 all-gather.8.cloned.1.call-update
  200.4 0.2 reduce-scatter.11.cloned.1.call-start
  200.7 22.6 %all-gather.8.cloned.1.call-done = bf16[256,2304]{0,1:T(8,128)(2,1)} async-done(((bf16[128,2304]{0,1:T(8,128)(2,1)}), bf16[256,2304]{0,1:T(8,128)(2,1)}) %all-gather.8.cloned.1.call-update) | async-done | bytes 1179664 | tf_op jit(solution)/shard_map/all_gather | solution.py:86
  223.3 15.8 %fusion.43 = f32[256,6144]{1,0:T(8,128)} fusion(bf16[256,2304]{0,1:T(8,128)(2,1)} %all-gather.8.cloned.1.call-done, bf16[6144,2304]{1,0:T(8,128)(2,1)} %param.7), kind=kOutput, calls=%fused_computation.62 | convolution fusion | flops 7247757312 | bytes 35782656 | tf_op jit(solution)/shard_map/dot_general | solution.py:92
  239.2 0.0 copy-start.3
  239.2 0.0 reduce-scatter.11.cloned.1.call-update
  239.2 1.1 copy-done.3
  240.3 0.0 copy-start.2
  240.3 0.4 convolution_convert_fusion.2
  240.7 7.5 %all_gather.19 = bf16[256,768]{0,1:T(8,128)(2,1)S(1)} all-gather(bf16[128,768]{0,1:T(8,128)(2,1)S(1)} %bitcast.62), channel_id=1, replica_groups=mesh['row'=2,'col'=8,'dp'=2] {'row'}, dimensions={0}, use_global_device_ids=true | all-gather | bytes 589824 | tf_op jit(solution)/shard_map/all_gather | solution.py:57
  248.2 0.0 copy-done.2
  248.2 0.0 copy-start.1
  248.2 5.1 %convolution_convert_fusion.1 = bf16[768,6144]{1,0:T(8,128)(2,1)} fusion(bf16[256,768]{0,1:T(8,128)(2,1)S(1)} %all_gather.19, bf16[256,6144]{1,0:T(8,128)(2,1)S(1)} %copy-done.2), kind=kOutput, calls=%fused_computation.3 | convolution fusion | flops 2420637696 | bytes 12976128 | tf_op jit(solution)/shard_map/dot_general | solution.py:61
  253.3 0.0 copy-done.1
  253.3 0.0 copy-start
  253.3 14.2 %convolution_convert_fusion = bf16[6144,2304]{1,0:T(8,128)(2,1)} fusion(bf16[256,6144]{1,0:T(8,128)(2,1)S(1)} %copy-done.1, bf16[256,2304]{0,1:T(8,128)(2,1)} %all-gather.8.cloned.1.call-done), kind=kOutput, calls=%fused_computation.2 | convolution fusion | flops 7261913088 | bytes 32636928 | tf_op jit(solution)/shard_map/dot_general | solution.py:87
  267.5 41.6 %reduce-scatter.11.cloned.1.call-done = f32[32,6144]{1,0:T(8,128)} async-done(((f32[256,6144]{1,0:T(8,128)}), f32[32,6144]{1,0:T(8,128)}) %reduce-scatter.11.cloned.1.call-update) | async-done | bytes 786448 | tf_op jit(solution)/shard_map/reduce_scatter | solution.py:91
  309.2 0.0 copy-done
  309.2 1.6 fusion.21
  310.7 26.6 %psum.39 = f32[6144]{0:T(1024)} all-reduce(f32[6144]{0:T(1024)S(1)} %get-tuple-element.4), channel_id=1, replica_groups=mesh['row'=2,'col'=8,'dp'=2] {'col'}, use_global_device_ids=true, to_apply=%region_16.17 | all-reduce | flops 6144 | bytes 49152 | tf_op jit(solution)/shard_map/psum | solution.py:97
  337.3 4.9 %all-reduce = (f32[32]{0:T(128)S(1)}, f32[32]{0:T(128)S(1)}) all-reduce(f32[32]{0:T(128)S(1)} %get-tuple-element.5, f32[32]{0:T(128)S(1)} %get-tuple-element.6), channel_id=1, replica_groups=mesh['row'=2,'col'=8,'dp'=2] {'row'}, use_global_device_ids=true, to_apply=%region_14.15 | all-reduce | flops 64 | bytes 512 | tf_op jit(solution)/shard_map/psum | solution.py:99
  342.2 2.2 fusion.20
  (5 shorter events, 0.1 us)
Async XLA Ops:
  7.2 43.5 %all-gather.6.cloned.1.call-start = ((), (), s32[]{:S(2)}) async-start(), calls=%async_computation.6 | async-start | bytes 3538944 | tf_op jit(solution)/shard_map/all_gather | solution.py:60
  7.9 82.2 %all-gather.4.cloned.1.call-start = ((), (), s32[]{:S(2)}) async-start(), calls=%async_computation.4 | async-start | bytes 3538944 | tf_op jit(solution)/shard_map/all_gather | solution.py:30
  23.1 86.1 %reduce-scatter.7.cloned.1.call-start = ((), (), s32[]{:S(2)}) async-start(), calls=%async_computation.7 | async-start | bytes 1179648 | tf_op jit(solution)/shard_map/reduce_scatter | solution.py:65
  58.8 87.9 %reduce-scatter.5.cloned.1.call-start = ((), (), s32[]{:S(2)}) async-start(), calls=%async_computation.5 | async-start | bytes 3538944 | tf_op jit(solution)/shard_map/reduce_scatter | solution.py:33
  105.5 92.7 %reduce-scatter.9.cloned.1.call-start = ((), (), s32[]{:S(2)}) async-start(), calls=%async_computation.8 | async-start | bytes 2359296 | tf_op jit(solution)/shard_map/reduce_scatter | solution.py:81
  172.0 51.3 %all-gather.8.cloned.1.call-start = ((), (), s32[]{:S(2)}) async-start(), calls=%async_computation.9 | async-start | bytes 1769472 | tf_op jit(solution)/shard_map/all_gather | solution.py:86
  200.4 108.7 %reduce-scatter.11.cloned.1.call-start = ((), (), s32[]{:S(2)}) async-start(), calls=%async_computation.10 | async-start | bytes 7077888 | tf_op jit(solution)/shard_map/reduce_scatter | solution.py:91
  239.2 1.1 copy-start.3
  240.3 7.9 %copy-start.2 = (bf16[256,6144]{1,0:T(8,128)(2,1)S(1)}, bf16[256,6144]{1,0:T(8,128)(2,1)}, u32[]{:S(2)}) copy-start(bf16[256,6144]{1,0:T(8,128)(2,1)} %all-gather.6.cloned.1.call-done) | copy-start | bytes 9437188
  248.2 5.1 %copy-start.1 = (bf16[256,6144]{1,0:T(8,128)(2,1)S(1)}, bf16[256,6144]{1,0:T(8,128)(2,1)}, u32[]{:S(2)}) copy-start(bf16[256,6144]{1,0:T(8,128)(2,1)} %all-gather.4.cloned.1.call-done) | copy-start | bytes 9437188
  253.3 55.8 %copy-start = (bf16[32,6144]{1,0:T(8,128)(2,1)S(1)}, bf16[32,6144]{1,0:T(8,128)(2,1)}, u32[]{:S(2)}) copy-start(bf16[32,6144]{1,0:T(8,128)(2,1)} %param.5) | copy-start | bytes 1179652
Sparse Core Ops, SparseCore 0:
  9.6 40.9 all-gather.5
  52.9 37.1 all-gather.3
  92.9 16.2 reduce-scatter.6
  112.0 34.6 reduce-scatter.4
  172.1 26.1 reduce-scatter.8
  200.6 22.7 all-gather.7
  239.3 69.8 reduce-scatter.10
where the time goes:
time: 352 us; the launch traced here: 351 us
  waiting for transfers between devices  184 us (52%)
  matrix products  74.6 us (21%)
  blocking collectives  61.3 us (17%)
  other arithmetic  14.2 us (4%)
  between operations  14.2 us (4%)
    reduce_scatter x1, waiting for transfers between devices, shards(): lax.psum_scatter(lax.dot_general(piece, w_qkv, (((1,), (1,)), ((), ())),...  41.6 us
    reduce_scatter x1, waiting for transfers between devices, shards(): lax.psum_scatter(jnp.dot(piece, w_qkv, preferred_element_type=jnp.float32...  36.3 us
    all_gather x1, waiting for transfers between devices, shards(): normed_all = lax.all_gather(normalized_output, 'col', axis=0, tiled=True)  31.2 us
    all_gather x1, waiting for transfers between devices, shards(): grad_all = lax.all_gather(out_grad, 'col', axis=0, tiled=True)  27.5 us
    psum x1, blocking collectives, shards(): lax.psum(jnp.sum(normalized_gradient * standardized_input, axis=0), 'col')  26.6 us
    all_gather x1, waiting for transfers between devices, shards(): d_qkv_all = lax.all_gather(owned_grad, 'row', axis=0, tiled=True)  22.6 us
    reduce_scatter x1, waiting for transfers between devices, shards(): lax.psum_scatter(d_pairs, 'row', scatter_dimension=0, tiled=True)  20.2 us
    dot_general x1, matrix products, shards(): lax.dot_general(piece, w_qkv, (((1,), (1,)), ((), ())), preferred_element...  15.8 us
  transfers between devices with their start and end apart: 7, of which 7 were waited for; matrix products, arithmetic and copies ran while one was open for 16% of the time, Pallas kernels for 0%

commit v1 on v0

--- a/solution.py
+++ b/solution.py
@@ -1,8 +1,11 @@
+import functools
 import math
 
 import jax
 import jax.numpy as jnp
 from jax import lax
+from jax.experimental import pallas as pl
+from jax.experimental.pallas import tpu as pltpu
 from jax.sharding import PartitionSpec as P
 
 HS = 128
@@ -107,6 +110,493 @@
     )
     return (input_gradient.astype(jnp.bfloat16), gain_gradient, grad_wqkv, grad_wout)
 
+MESH = pl.DeviceIdType.MESH
+F32 = jnp.float32
+BF16 = jnp.bfloat16
+NT = (((1,), (1,)), ((), ()))
+TN = (((0,), (0,)), ((), ()))
+NN = (((1,), (0,)), ((), ()))
+
+
+def mm(a, b, dims=NN):
+    return lax.dot_general(a, b, dims, preferred_element_type=F32)
+
+
+def block_kernel(
+    chips, x_ref, gain_ref, g_ref, wqkv_hbm, wout_hbm,
+    dx_ref, dgain_ref, n_out, g_out, ctx_out, dqkv_out,
+    wqkv, wout, nbuf, gbuf, xhat, rstd_buf, stat_send, stat_recv,
+    q_send, q_recv, qkv, probs, ctx, dc_send, dc_recv, dctx, dqkv,
+    acc, sib_send, sib_recv, z_send, z_recv, gg_send, gg_recv, total,
+    w_sem, out_sem, stat_ss, stat_rs, ag_up, ag_down, ag_recv, sib_ss, sib_rs,
+    q_ss, q_rs, c_ss, c_rs, dc_ss, dc_rs, dq_ss, dq_rs,
+    ps_ss, ps_rs, rs_ss, rs_rs, gg_ss, gg_rs,
+):
+    row = lax.axis_index("row")
+    col = lax.axis_index("col")
+    dp = lax.axis_index("dp")
+    z = col // 2
+    core = col % 2
+    rows, width = x_ref.shape
+    tokens = nbuf.shape[0]
+    own_heads = qkv.shape[0]
+    scale = 1.0 / math.sqrt(HS)
+    across = (1 - row, col, dp)
+    sibling = (row, z * 2 + 1 - core, dp)
+    above = (row, jnp.minimum(z + 1, chips - 1) * 2 + core, dp)
+    below = (row, jnp.maximum(z - 1, 0) * 2 + core, dp)
+    peers = 2 * chips
+
+    barrier = pltpu.get_barrier_semaphore()
+    pl.semaphore_signal(barrier, inc=1, device_id=across, device_id_type=MESH)
+    for k in range(1, peers):
+        pl.semaphore_signal(
+            barrier, inc=1, device_id=(row, (col + k) % peers, dp), device_id_type=MESH
+        )
+    load_qkv = pltpu.make_async_copy(wqkv_hbm, wqkv, w_sem.at[0])
+    load_out = pltpu.make_async_copy(wout_hbm, wout, w_sem.at[1])
+    load_qkv.start()
+    load_out.start()
+
+    x = x_ref[...].astype(F32)
+    mean_here = jnp.sum(x, axis=1, keepdims=True) / width
+    dev = x - mean_here
+    m2_here = jnp.sum(dev * dev, axis=1, keepdims=True)
+    stat_send[0, 0] = jnp.broadcast_to(mean_here, (rows, HS))
+    stat_send[0, 1] = jnp.broadcast_to(m2_here, (rows, HS))
+    gbuf[pl.ds(pl.multiple_of(col * rows, rows), rows), :] = g_ref[...]
+    pl.semaphore_wait(barrier, peers)
+
+    def remote(src, dst, ss, rs, device):
+        return pltpu.make_async_remote_copy(
+            src_ref=src, dst_ref=dst, send_sem=ss, recv_sem=rs, device_id=device, device_id_type=MESH
+        )
+
+    def slot(buf, chip, which):
+        return buf.at[pl.ds(pl.multiple_of((chip * 2 + which) * rows, rows), rows), :]
+
+    def z_copy(a, buf, b, up):
+        here = slot(buf, b, core)
+        ss = ag_up if up else ag_down
+        return remote(here, here, ss.at[a, b], ag_recv.at[a, b], above if up else below)
+
+    def s_copy(a, buf, b):
+        here = slot(buf, b, core)
+        return remote(here, here, sib_ss.at[a, b], sib_rs.at[a, b], sibling)
+
+    def gather_step(a, buf, d):
+        if d == 0:
+            @pl.when(z < chips - 1)
+            def _():
+                z_copy(a, buf, z, True).start()
+
+            @pl.when(z > 0)
+            def _():
+                z_copy(a, buf, z, False).start()
+
+            s_copy(a, buf, z).start()
+            return
+
+        @pl.when(z >= d)
+        def _():
+            z_copy(a, buf, z - d, True).wait_recv()
+
+            @pl.when(z < chips - 1)
+            def _():
+                z_copy(a, buf, z - d, True).start()
+
+            s_copy(a, buf, z - d).start()
+
+        @pl.when(z + d <= chips - 1)
+        def _():
+            z_copy(a, buf, z + d, False).wait_recv()
+
+            @pl.when(z > 0)
+            def _():
+                z_copy(a, buf, z + d, False).start()
+
+            s_copy(a, buf, z + d).start()
+
+    def gather_end(a, buf):
+        for b in range(chips):
+            there = slot(buf, b, 1 - core)
+            remote(there, there, sib_ss.at[a, b], sib_rs.at[a, b], sibling).wait_recv()
+
+    def gather_drain(a, buf):
+        for b in range(chips):
+            s_copy(a, buf, b).wait_send()
+
+            @pl.when((b <= z) & (z < chips - 1))
+            def _():
+                z_copy(a, buf, b, True).wait_send()
+
+            @pl.when((b >= z) & (z > 0))
+            def _():
+                z_copy(a, buf, b, False).wait_send()
+
+    gather_step(1, gbuf, 0)
+
+    stats = remote(stat_send.at[0], stat_recv.at[0], stat_ss.at[0], stat_rs.at[0], across)
+    stats.start()
+    stats.wait_recv()
+    mean_there = stat_recv[0, 0][:, :1]
+    m2_there = stat_recv[0, 1][:, :1]
+    gap = mean_here - mean_there
+    average = (mean_here + mean_there) * 0.5
+    variance = (m2_here + m2_there + gap * gap * (0.5 * width)) / (2.0 * width)
+    rstd = lax.rsqrt(variance + EPS)
+    rstd_buf[...] = jnp.broadcast_to(rstd, (rows, HS))
+    hat = (x_ref[...].astype(F32) - average) * rstd
+    xhat[...] = hat
+    nbuf[pl.ds(pl.multiple_of(col * rows, rows), rows), :] = (hat * gain_ref[...]).astype(BF16)
+
+    for d in range(chips):
+        gather_step(0, nbuf, d)
+        if d == chips - 2:
+            gather_step(1, gbuf, 1)
+    gather_end(0, nbuf)
+    save_n = pltpu.make_async_copy(nbuf, n_out, out_sem.at[0])
+    save_n.start()
+
+    load_qkv.wait()
+    wide = 3 * HS
+
+    def head_cols(r, i):
+        return pl.ds(pl.multiple_of((r * own_heads + i) * wide, HS), wide)
+
+    def q_copy(i):
+        return remote(q_send.at[i], q_recv.at[i], q_ss.at[i], q_rs.at[i], across)
+
+    deep = 1024
+
+    def pieces(k):
+        return pl.ds(pl.multiple_of(k * deep, deep), deep)
+
+    def project(cols):
+        total[...] = jnp.zeros_like(total)
+
+        def step(k, carry):
+            total[...] += mm(nbuf[:, pieces(k)], wqkv[pieces(k), cols])
+            return carry
+
+        lax.fori_loop(0, width // deep, step, 0)
+
+    def project_there(i, carry):
+        project(head_cols(1 - row, i))
+        q_send[i] = total[...].astype(BF16)
+        q_copy(i).start()
+        return carry
+
+    lax.fori_loop(0, own_heads, project_there, 0)
+    for d in range(2, chips):
+        gather_step(1, gbuf, d)
+        if d == 2:
+            def project_here(i, carry):
+                project(head_cols(row, i))
+                q_copy(i).wait_recv()
+                qkv[i] = (total[...] + q_recv[i].astype(F32)).astype(BF16)
+                return carry
+
+            lax.fori_loop(0, own_heads, project_here, 0)
+
+    allowed = lax.broadcasted_iota(jnp.int32, (tokens, tokens), 1) <= lax.broadcasted_iota(
+        jnp.int32, (tokens, tokens), 0
+    )
+
+    def ctx_copy(i):
+        here = ctx.at[row * own_heads + i]
+        return remote(here, here, c_ss.at[i], c_rs.at[i], across)
+
+    def forward(i, carry):
+        q = qkv[i, :, 0:HS]
+        k = qkv[i, :, HS:2 * HS]
+        v = qkv[i, :, 2 * HS:3 * HS]
+        s = jnp.where(allowed, mm(q, k, NT) * scale, -jnp.inf)
+        e = jnp.exp(s - jnp.max(s, axis=1, keepdims=True))
+        p = e / jnp.sum(e, axis=1, keepdims=True)
+        probs[i] = p
+        ctx[row * own_heads + i] = mm(p.astype(BF16), v).astype(BF16)
+        ctx_copy(i).start()
+        return carry
+
+    lax.fori_loop(0, own_heads, forward, 0)
+    gather_end(1, gbuf)
+    save_g = pltpu.make_async_copy(gbuf, g_out, out_sem.at[1])
+    save_g.start()
+
+    load_out.wait()
+    span = own_heads * HS
+
+    def out_rows(r):
+        return pl.ds(pl.multiple_of(r * span, HS), span)
+
+    def context_part(r):
+        total[...] = jnp.zeros_like(total)
+
+        def step(k, carry):
+            total[...] += mm(gbuf[:, pieces(k)], wout[out_rows(r), pieces(k)], NT)
+            return carry
+
+        lax.fori_loop(0, width // deep, step, 0)
+
+    context_part(1 - row)
+    dc_send[...] = total[...].astype(BF16)
+    dc_copy = remote(dc_send, dc_recv, dc_ss.at[0], dc_rs.at[0], across)
+    dc_copy.start()
+    context_part(row)
+    dc_copy.wait_recv()
+    dc = (total[...] + dc_recv[...].astype(F32)).astype(BF16)
+    for i in range(own_heads):
+        dctx[i] = dc[:, i * HS:(i + 1) * HS]
+
+    def dq_copy(i):
+        here = dqkv.at[:, head_cols(row, i)]
+        return remote(here, here, dq_ss.at[i], dq_rs.at[i], across)
+
+    def backward(i, carry):
+        q = qkv[i, :, 0:HS]
+        k = qkv[i, :, HS:2 * HS]
+        v = qkv[i, :, 2 * HS:3 * HS]
+        p = probs[i]
+        dch = dctx[i]
+        d_p = mm(dch, v, NT)
+        delta = jnp.sum(p * d_p, axis=1, keepdims=True)
+        d_s = (p * (d_p - delta) * scale).astype(BF16)
+        d_q = mm(d_s, k)
+        d_k = mm(d_s, q, TN)
+        d_v = mm(p.astype(BF16), dch, TN)
+        dqkv[:, head_cols(row, i)] = jnp.concatenate([d_q, d_k, d_v], axis=1).astype(BF16)
+        dq_copy(i).start()
+        return carry
+
+    lax.fori_loop(0, own_heads, backward, 0)
+    for i in range(own_heads):
+        there = dqkv.at[:, head_cols(1 - row, i)]
+        remote(there, there, dq_ss.at[i], dq_rs.at[i], across).wait_recv()
+        other = ctx.at[(1 - row) * own_heads + i]
+        remote(other, other, c_ss.at[i], c_rs.at[i], across).wait_recv()
+    save_dqkv = pltpu.make_async_copy(dqkv, dqkv_out, out_sem.at[2])
+    save_dqkv.start()
+    save_ctx = pltpu.make_async_copy(ctx, ctx_out, out_sem.at[3])
+    save_ctx.start()
+
+    tile = 256
+
+    def block_rows(b, which):
+        return dqkv[pl.ds(pl.multiple_of((b * 2 + which) * rows, rows), rows), :]
+
+    def partial_sums(b0, b1):
+        left = jnp.concatenate(
+            [block_rows(b0, core), block_rows(b1, core), block_rows(b0, 1 - core), block_rows(b1, 1 - core)],
+            axis=0,
+        )
+
+        def step(t, carry):
+            cols = pl.ds(pl.multiple_of(t * tile, tile), tile)
+            out = mm(left, wqkv[cols, :], NT)
+            acc[b0, :, cols] = out[0:rows]
+            acc[b1, :, cols] = out[rows:2 * rows]
+            sib_send[b0, :, cols] = out[2 * rows:3 * rows].astype(BF16)
+            sib_send[b1, :, cols] = out[3 * rows:].astype(BF16)
+            return carry
+
+        lax.fori_loop(0, width // tile, step, 0)
+        for b in (b0, b1):
+            pair_copy(b).start()
+
+    def pair_copy(b):
+        return remote(sib_send.at[b], sib_recv.at[b], ps_ss.at[b], ps_rs.at[b], sibling)
+
+    def line_copy(b, up):
+        w = 0 if up else 1
+        return remote(
+            z_send.at[b], z_recv.at[w, b], rs_ss.at[b], rs_rs.at[w, b], above if up else below
+        )
+
+    def hop(d):
+        @pl.when(z + d <= chips - 1)
+        def _():
+            b = z + d
+            z_send[b] = acc[b].astype(BF16)
+
+            @pl.when(z > 0)
+            def _():
+                line_copy(b, True).wait_recv()
+                z_send[b] = (acc[b] + z_recv[0, b].astype(F32)).astype(BF16)
+
+            line_copy(b, True).start()
+
+        @pl.when(z - d >= 0)
+        def _():
+            b = z - d
+            z_send[b] = acc[b].astype(BF16)
+
+            @pl.when(z < chips - 1)
+            def _():
+                line_copy(b, False).wait_recv()
+                z_send[b] = (acc[b] + z_recv[1, b].astype(F32)).astype(BF16)
+
+            line_copy(b, False).start()
+
+    def add_pair(b):
+        pair_copy(b).wait_recv()
+        acc[b] = acc[b] + sib_recv[b].astype(F32)
+
+    far = chips - 1
+    partial_sums(0, far)
+    add_pair(0)
+    add_pair(far)
+    hop(far)
+    partial_sums(1, 2)
+    add_pair(1)
+    add_pair(2)
+    for d in range(far - 1, 0, -1):
+        hop(d)
+
+    @pl.when(z > 0)
+    def _():
+        line_copy(z, True).wait_recv()
+        acc[z] = acc[z] + z_recv[0, z].astype(F32)
+
+    @pl.when(z < chips - 1)
+    def _():
+        line_copy(z, False).wait_recv()
+        acc[z] = acc[z] + z_recv[1, z].astype(F32)
+
+    dn = acc[z]
+    hat = xhat[...]
+    gg = jnp.sum(dn * hat, axis=0, keepdims=True)
+    gg_send[...] = gg
+
+    def gg_copy(k):
+        return remote(
+            gg_send, gg_recv.at[col], gg_ss.at[k], gg_rs.at[col], (row, (col + k) % peers, dp)
+        )
+
+    for k in range(1, peers):
+        gg_copy(k).start()
+    sg = dn * gain_ref[...]
+    first = jnp.sum(sg, axis=1, keepdims=True)
+    second = jnp.sum(sg * hat, axis=1, keepdims=True)
+    stat_send[1, 0] = jnp.broadcast_to(first, (rows, HS))
+    stat_send[1, 1] = jnp.broadcast_to(second, (rows, HS))
+    stats2 = remote(stat_send.at[1], stat_recv.at[1], stat_ss.at[1], stat_rs.at[1], across)
+    stats2.start()
+    stats2.wait_recv()
+    first = (first + stat_recv[1, 0][:, :1]) / (2.0 * width)
+    second = (second + stat_recv[1, 1][:, :1]) / (2.0 * width)
+    sg = acc[z] * gain_ref[...]
+    dx_ref[...] = (rstd_buf[:, :1] * (sg - first - xhat[...] * second)).astype(BF16)
+    gg_recv[col] = gg_send[...]
+    whole = jnp.zeros_like(gg)
+    for k in range(1, peers):
+        src = (col + k) % peers
+        remote(gg_send, gg_recv.at[src], gg_ss.at[k], gg_rs.at[src], (row, src, dp)).wait_recv()
+    for k in range(peers):
+        whole = whole + gg_recv[k]
+    dgain_ref[...] = whole
+
+    stats.wait_send()
+    stats2.wait_send()
+    gather_drain(0, nbuf)
+    gather_drain(1, gbuf)
+    for i in range(own_heads):
+        q_copy(i).wait_send()
+        ctx_copy(i).wait_send()
+        dq_copy(i).wait_send()
+    dc_copy.wait_send()
+    for b in range(chips):
+        pair_copy(b).wait_send()
+
+        @pl.when(b > z)
+        def _():
+            line_copy(b, True).wait_send()
+
+        @pl.when(b < z)
+        def _():
+            line_copy(b, False).wait_send()
+
+    for k in range(1, peers):
+        gg_copy(k).wait_send()
+    save_n.wait()
+    save_g.wait()
+    save_dqkv.wait()
+    save_ctx.wait()
+
+
+def pair_shards(layer_input, layer_norm_gain, w_qkv, w_out, out_grad):
+    rows, width = layer_input.shape
+    peers = lax.axis_size("col")
+    chips = peers // 2
+    tokens = rows * peers
+    columns = w_qkv.shape[1]
+    heads = columns // (3 * HS)
+    own = heads // 2
+    vmem = pl.BlockSpec(memory_space=pltpu.VMEM)
+    hbm = pl.BlockSpec(memory_space=pl.ANY)
+    dma = pltpu.SemaphoreType.DMA
+    shape = jax.ShapeDtypeStruct
+    dx, dgain, normed, grad, ctx, dqkv = pl.pallas_call(
+        functools.partial(block_kernel, chips),
+        out_shape=[
+            shape((rows, width), BF16),
+            shape((1, width), F32),
+            shape((tokens, width), BF16),
+            shape((tokens, width), BF16),
+            shape((heads, tokens, HS), BF16),
+            shape((tokens, columns), BF16),
+        ],
+        in_specs=[vmem, vmem, vmem, hbm, hbm],
+        out_specs=[vmem, vmem, hbm, hbm, hbm, hbm],
+        scratch_shapes=[
+            pltpu.VMEM(w_qkv.shape, BF16),
+            pltpu.VMEM(w_out.shape, BF16),
+            pltpu.VMEM((tokens, width), BF16),
+            pltpu.VMEM((tokens, width), BF16),
+            pltpu.VMEM((rows, width), F32),
+            pltpu.VMEM((rows, HS), F32),
+            pltpu.VMEM((2, 2, rows, HS), F32),
+            pltpu.VMEM((2, 2, rows, HS), F32),
+            pltpu.VMEM((own, tokens, 3 * HS), BF16),
+            pltpu.VMEM((own, tokens, 3 * HS), BF16),
+            pltpu.VMEM((own, tokens, 3 * HS), BF16),
+            pltpu.VMEM((own, tokens, tokens), F32),
+            pltpu.VMEM((heads, tokens, HS), BF16),
+            pltpu.VMEM((tokens, own * HS), BF16),
+            pltpu.VMEM((tokens, own * HS), BF16),
+            pltpu.VMEM((own, tokens, HS), BF16),
+            pltpu.VMEM((tokens, columns), BF16),
+            pltpu.VMEM((chips, rows, width), F32),
+            pltpu.VMEM((chips, rows, width), BF16),
+            pltpu.VMEM((chips, rows, width), BF16),
+            pltpu.VMEM((chips, rows, width), BF16),
+            pltpu.VMEM((2, chips, rows, width), BF16),
+            pltpu.VMEM((1, width), F32),
+            pltpu.VMEM((peers, 1, width), F32),
+            pltpu.VMEM((tokens, 3 * HS), F32),
+            dma((2,)), dma((4,)), dma((2,)), dma((2,)),
+            dma((2, chips)), dma((2, chips)), dma((2, chips)), dma((2, chips)), dma((2, chips)),
+            dma((own,)), dma((own,)), dma((own,)), dma((own,)),
+            dma((1,)), dma((1,)), dma((own,)), dma((own,)),
+            dma((chips,)), dma((chips,)), dma((chips,)), dma((2, chips)),
+            dma((peers,)), dma((peers,)),
+        ],
+        compiler_params=pltpu.CompilerParams(
+            collective_id=0, has_side_effects=True, vmem_limit_bytes=63 * 2**20
+        ),
+    )(layer_input, layer_norm_gain.reshape(1, width), out_grad, w_qkv, w_out)
+    grad_wqkv = mm(normed, dqkv, TN).astype(BF16)
+    context = ctx.transpose(1, 0, 2).reshape(tokens, heads * HS)
+    grad_wout = mm(context, grad, TN).astype(BF16)
+    return dx, dgain.reshape(width), grad_wqkv, grad_wout
+
+
+def choose(layer_input, layer_norm_gain, w_qkv, w_out, out_grad):
+    paired = lax.axis_size("row") == 2 and lax.axis_size("col") == 8
+    sized = layer_input.shape[1] % 1024 == 0 and layer_input.shape[0] == 32
+    body = pair_shards if paired and sized and w_qkv.shape[1] == 18 * HS else shards
+    return body(layer_input, layer_norm_gain, w_qkv, w_out, out_grad)
+
 
 def solution(mesh):
     in_specs = (
@@ -122,4 +612,4 @@
         P(("dp", "row"), "col"),
         P(("dp", "col"), "row"),
     )
-    return jax.shard_map(shards, mesh=mesh, in_specs=in_specs, out_specs=out_specs, check_vma=False)
+    return jax.shard_map(choose, mesh=mesh, in_specs=in_specs, out_specs=out_specs, check_vma=False)

time: 352 us -> 171 us (0.49)
  waiting for transfers between devices: 184 us -> 0 us
  Pallas kernels: 0 us -> 147 us
  blocking collectives: 61.3 us -> 0 us
  matrix products: 74.6 us -> 20.9 us
  other arithmetic: 14.2 us -> 0 us
  between operations: 14.2 us -> 0.68 us
    pallas_call x0 -> x1, Pallas kernels: none -> 147 us  [pair_shards(): pl.pallas_call(functools.partial(block_kernel, chips), out_shape=[shape((...]
    reduce_scatter x4 -> x0, waiting for transfers between devices: 102 us -> none  [the longest x1 41.6 us: shards(): lax.psum_scatter(lax.dot_general(piece, w_qkv, (((1,), (1,)), ((), ())),...]
    all_gather x3 -> x0, waiting for transfers between devices: 81.3 us -> none  [the longest x1 31.2 us: shards(): normed_all = lax.all_gather(normalized_output, 'col', axis=0, tiled=True)]
    dot_general x10 -> x2, matrix products: 73.3 us -> 20.9 us  [mm(): return lax.dot_general(a, b, dims, preferred_element_type=F32)]
    psum x4 -> x0, blocking collectives: 42.3 us -> none  [the longest x1 26.6 us: shards(): lax.psum(jnp.sum(normalized_gradient * standardized_input, axis=0), 'col')]
    all_gather x2 -> x0, blocking collectives: 19 us -> none  [the longest x1 11.5 us: shards(): key_value = lax.all_gather(owned[:, :, 1:], 'row', axis=0, tiled=True)]
    convert_element_type x5 -> x0, other arithmetic: 7.62 us -> none  [the longest x1 2.15 us: shards(): input_gradient.astype(jnp.bfloat16)]
    reduce_sum x3 -> x0, other arithmetic: 3.98 us -> none  [the longest x1 1.55 us: shards(): jnp.sum(normalized_gradient * standardized_input, axis=0)]
  transfers between devices with their start and end apart: 7 -> 0, of which waited for: 7 -> 0; matrix products, arithmetic and copies ran while one was open for 16% -> 0% of each run, Pallas kernels for 0% -> 0%
where the time goes in v1:
time: 171 us
  Pallas kernels  147 us (86%)
  matrix products  20.9 us (12%)
  local copies, waits for them, and re-layouts  2.53 us (1%)
    pallas_call x1, Pallas kernels, pair_shards(): pl.pallas_call(functools.partial(block_kernel, chips), out_shape=[shape((...  147 us
    dot_general x2, matrix products, mm(): return lax.dot_general(a, b, dims, preferred_element_type=F32)  20.9 us

profile of v1, /device:TPU:0, one launch (start us, length us, event | category | flops | bytes accessed | tf_op | source)
XLA Modules:
  0.0 171.0 jit_solution(2961081508374962445)
XLA Ops:
  0.6 146.9 %shard_map.84 = (bf16[32,6144]{1,0:T(8,128)(2,1)}, f32[1,6144]{1,0:T(1,128)}, bf16[256,6144]{1,0:T(8,128)(2,1)}, bf16[256,6144]{1,0:T(8,128)(2,1)}, bf16[6,256,1...) custom-call(bf16[32,6144]{1,0:T(8,128)(2,1)} %x_ref.1, f32[1,6144]{1,0:T(1,128)} %bitcast.10, bf16[32,6144]{1,0:T(8,128)(2,1)} %g_ref.1, ...), custom_call_target="tpu_custom_call" | custom-call | tf_op jit(solution)/shard_map/pallas_call | solution.py:539
  147.5 0.0 copy-start
  147.5 15.8 %convolution_convert_fusion = bf16[6144,2304]{1,0:T(8,128)(2,1)} fusion(bf16[256,6144]{1,0:T(8,128)(2,1)} %get-tuple-element.12, bf16[256,2304]{1,0:T(8,128)(2,1)} %get-tuple-element.13), kind=kOutput, calls=%fused_computation | convolution fusion | flops 7261913088 | bytes 32636928 | tf_op jit(solution)/shard_map/dot_general | solution.py:122
  163.3 1.2 copy.9
  164.5 0.0 copy-done
  164.5 0.0 copy-start.1
  164.5 0.0 copy-start.2
  164.5 5.2 %convolution_convert_fusion.1 = bf16[768,6144]{1,0:T(8,128)(2,1)} fusion(bf16[256,768]{0,1:T(8,128)(2,1)S(1)} %bitcast.8, bf16[256,6144]{1,0:T(8,128)(2,1)S(1)} %copy-done), kind=kOutput, calls=%fused_computation.1 | convolution fusion | flops 2420637696 | bytes 12976128 | tf_op jit(solution)/shard_map/dot_general | solution.py:122
  169.7 0.0 copy-done.1
  169.7 0.7 copy.12
  170.4 0.0 copy-done.2
  170.4 0.6 copy.13
Async XLA Ops:
  147.5 16.9 %copy-start = (bf16[256,6144]{1,0:T(8,128)(2,1)S(1)}, bf16[256,6144]{1,0:T(8,128)(2,1)}, u32[]{:S(2)}) copy-start(bf16[256,6144]{1,0:T(8,128)(2,1)} %get-tuple-element.15) | copy-start | bytes 9437188
  164.5 5.2 %copy-start.1 = (bf16[32,6144]{1,0:T(8,128)(2,1)S(1)}, bf16[32,6144]{1,0:T(8,128)(2,1)}, u32[]{:S(2)}) copy-start(bf16[32,6144]{1,0:T(8,128)(2,1)} %get-tuple-element.20) | copy-start | bytes 1179652
  164.5 5.9 %copy-start.2 = (f32[1,6144]{1,0:T(1,128)S(1)}, f32[1,6144]{1,0:T(1,128)}, u32[]{:S(2)}) copy-start(f32[1,6144]{1,0:T(1,128)} %get-tuple-element.11) | copy-start | bytes 73732

commit v2 on v1

--- a/solution.py
+++ b/solution.py
@@ -124,13 +124,13 @@
 
 def block_kernel(
     chips, x_ref, gain_ref, g_ref, wqkv_hbm, wout_hbm,
-    dx_ref, dgain_ref, n_out, g_out, ctx_out, dqkv_out,
+    n_out, g_out, ctx_out, dqkv_out, xhat_out, rstd_out, here_out, up_out, down_out, pass_out,
     wqkv, wout, nbuf, gbuf, xhat, rstd_buf, stat_send, stat_recv,
     q_send, q_recv, qkv, probs, ctx, dc_send, dc_recv, dctx, dqkv,
-    acc, sib_send, sib_recv, z_send, z_recv, gg_send, gg_recv, total,
-    w_sem, out_sem, stat_ss, stat_rs, ag_up, ag_down, ag_recv, sib_ss, sib_rs,
+    acc, sib_send, sib_recv, z_send, z_pass, z_recv, total,
+    w_sem, out_sem, ctx_sem, stat_ss, stat_rs, ag_up, ag_down, ag_recv, sib_ss, sib_rs,
     q_ss, q_rs, c_ss, c_rs, dc_ss, dc_rs, dq_ss, dq_rs,
-    ps_ss, ps_rs, rs_ss, rs_rs, gg_ss, gg_rs,
+    ps_ss, ps_rs, rs_ss, rs_rs,
 ):
     row = lax.axis_index("row")
     col = lax.axis_index("col")
@@ -377,8 +377,11 @@
         remote(other, other, c_ss.at[i], c_rs.at[i], across).wait_recv()
     save_dqkv = pltpu.make_async_copy(dqkv, dqkv_out, out_sem.at[2])
     save_dqkv.start()
-    save_ctx = pltpu.make_async_copy(ctx, ctx_out, out_sem.at[3])
-    save_ctx.start()
+    ctx_saves = []
+    for h in range(2 * own_heads):
+        to = ctx_out.at[:, h * HS:(h + 1) * HS]
+        ctx_saves.append(pltpu.make_async_copy(ctx.at[h], to, ctx_sem.at[h]))
+        ctx_saves[h].start()
 
     tile = 256
 
@@ -409,34 +412,18 @@
 
     def line_copy(b, up):
         w = 0 if up else 1
-        return remote(
-            z_send.at[b], z_recv.at[w, b], rs_ss.at[b], rs_rs.at[w, b], above if up else below
-        )
-
-    def hop(d):
-        @pl.when(z + d <= chips - 1)
+        return remote(z_send, z_recv.at[w], rs_ss.at[w], rs_rs.at[w], above if up else below)
+
+    def hop_far():
+        @pl.when(z == 0)
         def _():
-            b = z + d
-            z_send[b] = acc[b].astype(BF16)
-
-            @pl.when(z > 0)
-            def _():
-                line_copy(b, True).wait_recv()
-                z_send[b] = (acc[b] + z_recv[0, b].astype(F32)).astype(BF16)
-
-            line_copy(b, True).start()
-
-        @pl.when(z - d >= 0)
+            z_send[...] = acc[far].astype(BF16)
+            line_copy(far, True).start()
+
+        @pl.when(z == far)
         def _():
-            b = z - d
-            z_send[b] = acc[b].astype(BF16)
-
-            @pl.when(z < chips - 1)
-            def _():
-                line_copy(b, False).wait_recv()
-                z_send[b] = (acc[b] + z_recv[1, b].astype(F32)).astype(BF16)
-
-            line_copy(b, False).start()
+            z_send[...] = acc[0].astype(BF16)
+            line_copy(0, False).start()
 
     def add_pair(b):
         pair_copy(b).wait_recv()
@@ -446,58 +433,37 @@
     partial_sums(0, far)
     add_pair(0)
     add_pair(far)
-    hop(far)
+    hop_far()
     partial_sums(1, 2)
     add_pair(1)
     add_pair(2)
-    for d in range(far - 1, 0, -1):
-        hop(d)
-
-    @pl.when(z > 0)
+
+    half = chips // 2
+    b_pass = jnp.where(z < half, z + half, z - half)
+    z_pass[...] = acc[b_pass].astype(BF16)
+
+    @pl.when(z == 1)
     def _():
-        line_copy(z, True).wait_recv()
-        acc[z] = acc[z] + z_recv[0, z].astype(F32)
-
-    @pl.when(z < chips - 1)
+        line_copy(far, True).wait_recv()
+        z_pass[...] = (acc[far] + z_recv[0].astype(F32)).astype(BF16)
+
+    @pl.when(z == far - 1)
     def _():
-        line_copy(z, False).wait_recv()
-        acc[z] = acc[z] + z_recv[1, z].astype(F32)
-
-    dn = acc[z]
-    hat = xhat[...]
-    gg = jnp.sum(dn * hat, axis=0, keepdims=True)
-    gg_send[...] = gg
-
-    def gg_copy(k):
-        return remote(
-            gg_send, gg_recv.at[col], gg_ss.at[k], gg_rs.at[col], (row, (col + k) % peers, dp)
-        )
-
-    for k in range(1, peers):
-        gg_copy(k).start()
-    sg = dn * gain_ref[...]
-    first = jnp.sum(sg, axis=1, keepdims=True)
-    second = jnp.sum(sg * hat, axis=1, keepdims=True)
-    stat_send[1, 0] = jnp.broadcast_to(first, (rows, HS))
-    stat_send[1, 1] = jnp.broadcast_to(second, (rows, HS))
-    stats2 = remote(stat_send.at[1], stat_recv.at[1], stat_ss.at[1], stat_rs.at[1], across)
-    stats2.start()
-    stats2.wait_recv()
-    first = (first + stat_recv[1, 0][:, :1]) / (2.0 * width)
-    second = (second + stat_recv[1, 1][:, :1]) / (2.0 * width)
-    sg = acc[z] * gain_ref[...]
-    dx_ref[...] = (rstd_buf[:, :1] * (sg - first - xhat[...] * second)).astype(BF16)
-    gg_recv[col] = gg_send[...]
-    whole = jnp.zeros_like(gg)
-    for k in range(1, peers):
-        src = (col + k) % peers
-        remote(gg_send, gg_recv.at[src], gg_ss.at[k], gg_rs.at[src], (row, src, dp)).wait_recv()
-    for k in range(peers):
-        whole = whole + gg_recv[k]
-    dgain_ref[...] = whole
+        line_copy(0, False).wait_recv()
+        z_pass[...] = (acc[0] + z_recv[1].astype(F32)).astype(BF16)
+
+    saves = [
+        pltpu.make_async_copy(xhat, xhat_out, out_sem.at[4]),
+        pltpu.make_async_copy(rstd_buf, rstd_out, out_sem.at[5]),
+        pltpu.make_async_copy(acc.at[z], here_out, out_sem.at[6]),
+        pltpu.make_async_copy(acc.at[jnp.minimum(z + 1, far)], up_out, out_sem.at[7]),
+        pltpu.make_async_copy(acc.at[jnp.maximum(z - 1, 0)], down_out, out_sem.at[8]),
+        pltpu.make_async_copy(z_pass, pass_out, out_sem.at[9]),
+    ]
+    for save in saves:
+        save.start()
 
     stats.wait_send()
-    stats2.wait_send()
     gather_drain(0, nbuf)
     gather_drain(1, gbuf)
     for i in range(own_heads):
@@ -508,20 +474,79 @@
     for b in range(chips):
         pair_copy(b).wait_send()
 
-        @pl.when(b > z)
-        def _():
-            line_copy(b, True).wait_send()
-
-        @pl.when(b < z)
-        def _():
-            line_copy(b, False).wait_send()
-
-    for k in range(1, peers):
-        gg_copy(k).wait_send()
+    @pl.when(z == 0)
+    def _():
+        line_copy(far, True).wait_send()
+
+    @pl.when(z == far)
+    def _():
+        line_copy(0, False).wait_send()
+
     save_n.wait()
     save_g.wait()
     save_dqkv.wait()
-    save_ctx.wait()
+    for save in saves:
+        save.wait()
+    for save in ctx_saves:
+        save.wait()
+
+
+def norm_kernel(
+    here_ref, from_below, from_above, xhat_ref, rstd_ref, gain_ref, dx_ref, dgain_ref,
+    dn_buf, stat_send, stat_recv, gg_send, gg_recv, stat_ss, stat_rs, gg_ss, gg_rs,
+):
+    row = lax.axis_index("row")
+    col = lax.axis_index("col")
+    dp = lax.axis_index("dp")
+    rows, width = here_ref.shape
+    peers = gg_recv.shape[0]
+    across = (1 - row, col, dp)
+
+    barrier = pltpu.get_barrier_semaphore()
+    pl.semaphore_signal(barrier, inc=1, device_id=across, device_id_type=MESH)
+    for k in range(1, peers):
+        pl.semaphore_signal(
+            barrier, inc=1, device_id=(row, (col + k) % peers, dp), device_id_type=MESH
+        )
+    dn = here_ref[...] + from_below[...].astype(F32) + from_above[...].astype(F32)
+    sg = dn * gain_ref[...]
+    dn_buf[...] = sg
+    hat = xhat_ref[...]
+    first = jnp.sum(sg, axis=1, keepdims=True)
+    second = jnp.sum(sg * hat, axis=1, keepdims=True)
+    stat_send[0] = jnp.broadcast_to(first, (rows, HS))
+    stat_send[1] = jnp.broadcast_to(second, (rows, HS))
+    gg_send[...] = jnp.sum(dn * hat, axis=0, keepdims=True)
+    pl.semaphore_wait(barrier, peers)
+
+    stats = pltpu.make_async_remote_copy(
+        src_ref=stat_send, dst_ref=stat_recv, send_sem=stat_ss.at[0], recv_sem=stat_rs.at[0],
+        device_id=across, device_id_type=MESH,
+    )
+    stats.start()
+
+    def gg_copy(k, source):
+        return pltpu.make_async_remote_copy(
+            src_ref=gg_send, dst_ref=gg_recv.at[source], send_sem=gg_ss.at[k], recv_sem=gg_rs.at[source],
+            device_id=(row, (col + k) % peers, dp), device_id_type=MESH,
+        )
+
+    for k in range(1, peers):
+        gg_copy(k, col).start()
+    stats.wait_recv()
+    first = (first + stat_recv[0][:, :1]) / (2.0 * width)
+    second = (second + stat_recv[1][:, :1]) / (2.0 * width)
+    dx_ref[...] = (rstd_ref[:, :1] * (dn_buf[...] - first - xhat_ref[...] * second)).astype(BF16)
+    gg_recv[col] = gg_send[...]
+    for k in range(1, peers):
+        gg_copy(k, (col + k) % peers).wait_recv()
+    whole = gg_recv[0]
+    for k in range(1, peers):
+        whole = whole + gg_recv[k]
+    dgain_ref[...] = whole
+    stats.wait_send()
+    for k in range(1, peers):
+        gg_copy(k, col).wait_send()
 
 
 def pair_shards(layer_input, layer_norm_gain, w_qkv, w_out, out_grad):
@@ -536,18 +561,22 @@
     hbm = pl.BlockSpec(memory_space=pl.ANY)
     dma = pltpu.SemaphoreType.DMA
     shape = jax.ShapeDtypeStruct
-    dx, dgain, normed, grad, ctx, dqkv = pl.pallas_call(
+    normed, grad, context, dqkv, xhat, rstd, here, up, down, onward = pl.pallas_call(
         functools.partial(block_kernel, chips),
         out_shape=[
-            shape((rows, width), BF16),
-            shape((1, width), F32),
             shape((tokens, width), BF16),
             shape((tokens, width), BF16),
-            shape((heads, tokens, HS), BF16),
+            shape((tokens, heads * HS), BF16),
             shape((tokens, columns), BF16),
+            shape((rows, width), F32),
+            shape((rows, HS), F32),
+            shape((rows, width), F32),
+            shape((rows, width), F32),
+            shape((rows, width), F32),
+            shape((rows, width), BF16),
         ],
         in_specs=[vmem, vmem, vmem, hbm, hbm],
-        out_specs=[vmem, vmem, hbm, hbm, hbm, hbm],
+        out_specs=[hbm] * 10,
         scratch_shapes=[
             pltpu.VMEM(w_qkv.shape, BF16),
             pltpu.VMEM(w_out.shape, BF16),
@@ -555,8 +584,8 @@
             pltpu.VMEM((tokens, width), BF16),
             pltpu.VMEM((rows, width), F32),
             pltpu.VMEM((rows, HS), F32),
-            pltpu.VMEM((2, 2, rows, HS), F32),
-            pltpu.VMEM((2, 2, rows, HS), F32),
+            pltpu.VMEM((1, 2, rows, HS), F32),
+            pltpu.VMEM((1, 2, rows, HS), F32),
             pltpu.VMEM((own, tokens, 3 * HS), BF16),
             pltpu.VMEM((own, tokens, 3 * HS), BF16),
             pltpu.VMEM((own, tokens, 3 * HS), BF16),
@@ -569,25 +598,51 @@
             pltpu.VMEM((chips, rows, width), F32),
             pltpu.VMEM((chips, rows, width), BF16),
             pltpu.VMEM((chips, rows, width), BF16),
-            pltpu.VMEM((chips, rows, width), BF16),
-            pltpu.VMEM((2, chips, rows, width), BF16),
-            pltpu.VMEM((1, width), F32),
-            pltpu.VMEM((peers, 1, width), F32),
+            pltpu.VMEM((rows, width), BF16),
+            pltpu.VMEM((rows, width), BF16),
+            pltpu.VMEM((2, rows, width), BF16),
             pltpu.VMEM((tokens, 3 * HS), F32),
-            dma((2,)), dma((4,)), dma((2,)), dma((2,)),
+            dma((2,)), dma((10,)), dma((heads,)), dma((1,)), dma((1,)),
             dma((2, chips)), dma((2, chips)), dma((2, chips)), dma((2, chips)), dma((2, chips)),
             dma((own,)), dma((own,)), dma((own,)), dma((own,)),
             dma((1,)), dma((1,)), dma((own,)), dma((own,)),
-            dma((chips,)), dma((chips,)), dma((chips,)), dma((2, chips)),
-            dma((peers,)), dma((peers,)),
+            dma((chips,)), dma((chips,)), dma((2,)), dma((2,)),
         ],
         compiler_params=pltpu.CompilerParams(
             collective_id=0, has_side_effects=True, vmem_limit_bytes=63 * 2**20
         ),
     )(layer_input, layer_norm_gain.reshape(1, width), out_grad, w_qkv, w_out)
+    half = chips // 2
+    both = range(2)
+    rise = [(2 * z + c, 2 * z + 2 + c) for z in range(chips - 1) for c in both]
+    fall = [(b, a) for a, b in rise]
+    rise_first = [(2 * z + c, 2 * z + 2 + c) for z in range(half) for c in both]
+    fall_first = [(2 * z + c, 2 * z - 2 + c) for z in range(half, chips) for c in both]
+    got_up = lax.ppermute(onward, "col", rise_first)
+    got_down = lax.ppermute(onward, "col", fall_first)
     grad_wqkv = mm(normed, dqkv, TN).astype(BF16)
-    context = ctx.transpose(1, 0, 2).reshape(tokens, heads * HS)
+    next_up = (up + got_up.astype(F32)).astype(BF16)
+    next_down = (down + got_down.astype(F32)).astype(BF16)
+    from_below = lax.ppermute(next_up, "col", rise)
+    from_above = lax.ppermute(next_down, "col", fall)
     grad_wout = mm(context, grad, TN).astype(BF16)
+    dx, dgain = pl.pallas_call(
+        norm_kernel,
+        out_shape=[shape((rows, width), BF16), shape((1, width), F32)],
+        in_specs=[vmem] * 6,
+        out_specs=[vmem] * 2,
+        scratch_shapes=[
+            pltpu.VMEM((rows, width), F32),
+            pltpu.VMEM((2, rows, HS), F32),
+            pltpu.VMEM((2, rows, HS), F32),
+            pltpu.VMEM((1, width), F32),
+            pltpu.VMEM((peers, 1, width), F32),
+            dma((1,)), dma((1,)), dma((peers,)), dma((peers,)),
+        ],
+        compiler_params=pltpu.CompilerParams(
+            collective_id=1, has_side_effects=True, vmem_limit_bytes=24 * 2**20
+        ),
+    )(here, from_below, from_above, xhat, rstd, layer_norm_gain.reshape(1, width))
     return dx, dgain.reshape(width), grad_wqkv, grad_wout
 
 

time: 171 us -> 165 us (0.965)
  Pallas kernels: 147 us -> 130 us
  starting transfers between devices: 0 us -> 8.13 us
  waiting for transfers between devices: 0 us -> 2.35 us
    pallas_call x1, Pallas kernels: 147 us -> 123 us  [pair_shards(): pl.pallas_call(functools.partial(block_kernel, chips), out_shape=[shape((...]
    ppermute x0 -> x4, starting transfers between devices: none -> 8.13 us  [the longest x1 4.57 us: pair_shards(): from_below = lax.ppermute(next_up, 'col', rise)]
    pallas_call x0 -> x1, Pallas kernels: none -> 7.22 us  [pair_shards(): pl.pallas_call(norm_kernel, out_shape=[shape((rows, width), BF16), shape(...]
    ppermute x0 -> x4, waiting for transfers between devices: none -> 2.35 us  [the longest x1 1.28 us: pair_shards(): from_below = lax.ppermute(next_up, 'col', rise)]
  transfers between devices with their start and end apart: 0 -> 4, of which waited for: 0 -> 2; matrix products, arithmetic and copies ran while one was open for 0% -> 13% of each run, Pallas kernels for 0% -> 0%
where the time goes in v2:
time: 165 us; the launch traced here: 164 us
  Pallas kernels  130 us (79%)
  matrix products  20.9 us (13%)
  starting transfers between devices  8.13 us (5%)
  waiting for transfers between devices  2.35 us (1%)
    pallas_call x1, Pallas kernels, pair_shards(): pl.pallas_call(functools.partial(block_kernel, chips), out_shape=[shape((...  123 us
    dot_general x2, matrix products, mm(): return lax.dot_general(a, b, dims, preferred_element_type=F32)  20.9 us
    pallas_call x1, Pallas kernels, pair_shards(): pl.pallas_call(norm_kernel, out_shape=[shape((rows, width), BF16), shape(...  7.22 us
    ppermute x1, starting transfers between devices, pair_shards(): from_below = lax.ppermute(next_up, 'col', rise)  4.57 us
  transfers between devices with their start and end apart: 4, of which 2 were waited for; matrix products, arithmetic and copies ran while one was open for 13% of the time, Pallas kernels for 0%

profile of v2, /device:TPU:0, one launch (start us, length us, event | category | flops | bytes accessed | tf_op | source)
XLA Modules:
  0.0 163.8 jit_solution(16310504653568359634)
XLA Ops:
  0.6 122.9 %shard_map.84 = (bf16[256,6144]{1,0:T(8,128)(2,1)}, bf16[256,6144]{1,0:T(8,128)(2,1)}, bf16[256,768]{1,0:T(8,128)(2,1)}, bf16[256,2304]{1,0:T(8,128)(2,1)}, f32[...) custom-call(bf16[32,6144]{1,0:T(8,128)(2,1)} %x_ref.1, ...), custom_call_target="tpu_custom_call" | custom-call | tf_op jit(solution)/shard_map/pallas_call | solution.py:564
  123.5 0.7 collective-permute-start.2
  124.2 1.3 collective-permute-start
  125.5 0.0 copy-start.6
  125.5 0.0 copy-start.5
  125.5 0.0 copy-start.7
  125.5 15.7 %convolution_convert_fusion = bf16[6144,2304]{1,0:T(8,128)(2,1)} fusion(bf16[256,6144]{1,0:T(8,128)(2,1)} %get-tuple-element.24, bf16[256,2304]{1,0:T(8,128)(2,1)} %get-tuple-element.25), kind=kOutput, calls=%fused_computation | convolution fusion | flops 7261913088 | bytes 32636928 | tf_op jit(solution)/shard_map/dot_general | solution.py:122
  141.3 0.0 copy-start.4
  141.3 0.0 collective-permute-done.2
  141.3 0.0 copy-done.6
  141.3 0.1 add_convert_fusion
  141.4 1.6 collective-permute-start.3
  142.9 0.0 collective-permute-done
  142.9 0.0 copy-done.5
  143.0 0.1 add_convert_fusion.1
  143.0 4.6 %collective-permute-start.1 = (bf16[32,6144]{1,0:T(8,128)(2,1)S(1)}, bf16[32,6144]{1,0:T(8,128)(2,1)S(1)}, u32[]{:S(2)}, u32[]{:S(2)}) collective-permute-start(bf16[32,6144]{1,0:T(8,128)(2,1)S(1)} %add_convert_fusion.1), channel_id=1, source_target_pairs={{0,4},{2,6},{4,8},{6,10},{8,12},{10,14},{1,5},{3,7},{5,9},{7,11},{... | collective-permute-start | bytes 1179656 | tf_op jit(solution)/shard_map/ppermute | solution.py:626
  147.6 0.0 copy-done.7
  147.6 0.0 copy-done.4
  147.6 0.0 copy-start
  147.6 0.0 copy-start.1
  147.7 0.0 copy-start.2
  147.7 0.0 copy-start.3
  147.7 5.2 %convolution_convert_fusion.1 = bf16[768,6144]{1,0:T(8,128)(2,1)} fusion(bf16[256,768]{1,0:T(8,128)(2,1)S(1)} %copy-done.7, bf16[256,6144]{1,0:T(8,128)(2,1)S(1)} %copy-done.4), kind=kOutput, calls=%fused_computation.1 | convolution fusion | flops 2420637696 | bytes 12976128 | tf_op jit(solution)/shard_map/dot_general | solution.py:122
  152.9 1.1 collective-permute-done.3.from_above
  153.9 1.3 collective-permute-done.1.from_below
  155.2 0.0 copy-done
  155.2 0.0 copy-done.1
  155.2 0.0 copy-done.2
  155.2 0.0 copy-done.3
  155.2 7.2 %shard_map.85 = (bf16[32,6144]{1,0:T(8,128)(2,1)S(1)}, f32[1,6144]{1,0:T(1,128)S(1)}) custom-call(f32[32,6144]{1,0:T(8,128)S(1)} %copy-done.1, bf16[32,6144]{1,0:T(8,128)(2,1)S(1)} %collective-permute-done.1.from_below, bf16[32,6144]{1,0:T(8,128)(2,1)S(1)} %collective-permute-done.3.from_above, f32[32,6144]{1,0:T(8,128)S(1)} %copy-done, ...), custom_call_target="tpu_custom_call" | custom-call | tf_op jit(solution)/shard_map/pallas_call | solution.py:629
  162.4 0.7 copy.11
  163.2 0.6 copy.12
Async XLA Ops:
  123.5 17.8 %collective-permute-start.2 = (bf16[32,6144]{1,0:T(8,128)(2,1)}, bf16[32,6144]{1,0:T(8,128)(2,1)S(1)}, u32[]{:S(2)}, u32[]{:S(2)}) collective-permute-start(bf16[32,6144]{1,0:T(8,128)(2,1)} %get-tuple-element.18), channel_id=1, source_target_pairs={{8,4},{10,6},{12,8},{14,10},{9,5},{11,7},{13,9},{15,11},{24,20},{2... | collective-permute-start | bytes 1179656 | tf_op jit(solution)/shard_map/ppermute | solution.py:622
  124.2 18.8 %collective-permute-start = (bf16[32,6144]{1,0:T(8,128)(2,1)}, bf16[32,6144]{1,0:T(8,128)(2,1)S(1)}, u32[]{:S(2)}, u32[]{:S(2)}) collective-permute-start(bf16[32,6144]{1,0:T(8,128)(2,1)} %get-tuple-element.18), channel_id=1, source_target_pairs={{0,4},{2,6},{4,8},{6,10},{1,5},{3,7},{5,9},{7,11},{16,20},{18,22},... | collective-permute-start | bytes 1179656 | tf_op jit(solution)/shard_map/ppermute | solution.py:621
  125.5 15.8 %copy-start.6 = (f32[32,6144]{1,0:T(8,128)S(1)}, f32[32,6144]{1,0:T(8,128)}, u32[]{:S(2)}) copy-start(f32[32,6144]{1,0:T(8,128)} %get-tuple-element.19) | copy-start | bytes 2359300
  125.5 17.4 %copy-start.5 = (f32[32,6144]{1,0:T(8,128)S(1)}, f32[32,6144]{1,0:T(8,128)}, u32[]{:S(2)}) copy-start(f32[32,6144]{1,0:T(8,128)} %get-tuple-element.17) | copy-start | bytes 2359300
  125.5 22.1 %copy-start.7 = (bf16[256,768]{1,0:T(8,128)(2,1)S(1)}, bf16[256,768]{1,0:T(8,128)(2,1)}, u32[]{:S(2)}) copy-start(bf16[256,768]{1,0:T(8,128)(2,1)} %get-tuple-element.26) | copy-start | bytes 1179652
  141.3 6.3 %copy-start.4 = (bf16[256,6144]{1,0:T(8,128)(2,1)S(1)}, bf16[256,6144]{1,0:T(8,128)(2,1)}, u32[]{:S(2)}) copy-start(bf16[256,6144]{1,0:T(8,128)(2,1)} %get-tuple-element.27) | copy-start | bytes 9437188
  141.4 12.6 %collective-permute-start.3 = (bf16[32,6144]{1,0:T(8,128)(2,1)S(1)}, bf16[32,6144]{1,0:T(8,128)(2,1)S(1)}, u32[]{:S(2)}, u32[]{:S(2)}) collective-permute-start(bf16[32,6144]{1,0:T(8,128)(2,1)S(1)} %add_convert_fusion), channel_id=1, source_target_pairs={{4,0},{6,2},{8,4},{10,6},{12,8},{14,10},{5,1},{7,3},{9,5},{11,7},{... | collective-permute-start | bytes 1179656 | tf_op jit(solution)/shard_map/ppermute | solution.py:627
  143.0 12.2 %collective-permute-start.1 = (bf16[32,6144]{1,0:T(8,128)(2,1)S(1)}, bf16[32,6144]{1,0:T(8,128)(2,1)S(1)}, u32[]{:S(2)}, u32[]{:S(2)}) collective-permute-start(bf16[32,6144]{1,0:T(8,128)(2,1)S(1)} %add_convert_fusion.1), channel_id=1, source_target_pairs={{0,4},{2,6},{4,8},{6,10},{8,12},{10,14},{1,5},{3,7},{5,9},{7,11},{... | collective-permute-start | bytes 1179656 | tf_op jit(solution)/shard_map/ppermute | solution.py:626
  147.6 7.6 %copy-start = (f32[32,6144]{1,0:T(8,128)S(1)}, f32[32,6144]{1,0:T(8,128)}, u32[]{:S(2)}) copy-start(f32[32,6144]{1,0:T(8,128)} %get-tuple-element.20.xhat_ref) | copy-start | bytes 2359300
  147.6 7.6 %copy-start.1 = (f32[32,6144]{1,0:T(8,128)S(1)}, f32[32,6144]{1,0:T(8,128)}, u32[]{:S(2)}) copy-start(f32[32,6144]{1,0:T(8,128)} %get-tuple-element.16.here_ref) | copy-start | bytes 2359300
  147.7 7.6 %copy-start.2 = (f32[6144]{0:T(1024)S(1)}, f32[6144]{0:T(1024)}, u32[]{:S(2)}) copy-start(f32[6144]{0:T(1024)} %param.6) | copy-start | bytes 73732
  147.7 7.6 %copy-start.3 = (f32[32,128]{1,0:T(8,128)S(1)}, f32[32,128]{1,0:T(8,128)}, u32[]{:S(2)}) copy-start(f32[32,128]{1,0:T(8,128)} %get-tuple-element.21.rstd_ref) | copy-start | bytes 49156

commit v3 on v2

--- a/solution.py
+++ b/solution.py
@@ -127,7 +127,7 @@
     n_out, g_out, ctx_out, dqkv_out, xhat_out, rstd_out, here_out, up_out, down_out, pass_out,
     wqkv, wout, nbuf, gbuf, xhat, rstd_buf, stat_send, stat_recv,
     q_send, q_recv, qkv, probs, ctx, dc_send, dc_recv, dctx, dqkv,
-    acc, sib_send, sib_recv, z_send, z_pass, z_recv, total,
+    acc, sib_send, sib_recv, z_send, z_pass, z_recv, total, own_part,
     w_sem, out_sem, ctx_sem, stat_ss, stat_rs, ag_up, ag_down, ag_recv, sib_ss, sib_rs,
     q_ss, q_rs, c_ss, c_rs, dc_ss, dc_rs, dq_ss, dq_rs,
     ps_ss, ps_rs, rs_ss, rs_rs,
@@ -217,10 +217,9 @@
 
             s_copy(a, buf, z + d).start()
 
-    def gather_end(a, buf):
-        for b in range(chips):
-            there = slot(buf, b, 1 - core)
-            remote(there, there, sib_ss.at[a, b], sib_rs.at[a, b], sibling).wait_recv()
+    def pair_wait(a, buf, b):
+        there = slot(buf, b, 1 - core)
+        remote(there, there, sib_ss.at[a, b], sib_rs.at[a, b], sibling).wait_recv()
 
     def gather_drain(a, buf):
         for b in range(chips):
@@ -250,54 +249,79 @@
     xhat[...] = hat
     nbuf[pl.ds(pl.multiple_of(col * rows, rows), rows), :] = (hat * gain_ref[...]).astype(BF16)
 
-    for d in range(chips):
-        gather_step(0, nbuf, d)
-        if d == chips - 2:
-            gather_step(1, gbuf, 1)
-    gather_end(0, nbuf)
+    wide = 3 * HS
+    deep = 1024
+    chip_rows = 2 * rows
+    low = z < chips // 2
+    near = jnp.where(low, 0, 2)
+    third = jnp.where(low, 2, 1)
+    last = jnp.where(low, 3, 0)
+
+    def head_cols(r, i):
+        return pl.ds(pl.multiple_of((r * own_heads + i) * wide, HS), wide)
+
+    def pieces(k):
+        return pl.ds(pl.multiple_of(k * deep, deep), deep)
+
+    def chip_span(b, count):
+        return pl.ds(pl.multiple_of(b * chip_rows, chip_rows), count * chip_rows)
+
+    spans = [(chip_span(near, 2), 2 * chip_rows), (chip_span(third, 1), chip_rows), (chip_span(last, 1), chip_rows)]
+
+    def q_copy(i, j):
+        here = spans[j][0]
+        return remote(q_send.at[i, here], q_recv.at[i, here], q_ss.at[j, i], q_rs.at[j, i], across)
+
+    def project_piece(j):
+        here, count = spans[j]
+
+        def project(cols):
+            total[0:count] = jnp.zeros((count, wide), F32)
+
+            def step(k, carry):
+                total[0:count] += mm(nbuf[here, pieces(k)], wqkv[pieces(k), cols])
+                return carry
+
+            lax.fori_loop(0, width // deep, step, 0)
+
+        def there(i, carry):
+            project(head_cols(1 - row, i))
+            q_send[i, here] = total[0:count].astype(BF16)
+            q_copy(i, j).start()
+            return carry
+
+        def own(i, carry):
+            project(head_cols(row, i))
+            own_part[i, here] = total[0:count]
+            return carry
+
+        lax.fori_loop(0, own_heads, there, 0)
+        lax.fori_loop(0, own_heads, own, 0)
+
+    gather_step(0, nbuf, 0)
+    gather_step(0, nbuf, 1)
+    load_qkv.wait()
+    pair_wait(0, nbuf, near)
+    pair_wait(0, nbuf, near + 1)
+    project_piece(0)
+    gather_step(0, nbuf, 2)
+    gather_step(1, gbuf, 1)
+    pair_wait(0, nbuf, third)
+    project_piece(1)
+    gather_step(0, nbuf, 3)
+    pair_wait(0, nbuf, last)
     save_n = pltpu.make_async_copy(nbuf, n_out, out_sem.at[0])
     save_n.start()
-
-    load_qkv.wait()
-    wide = 3 * HS
-
-    def head_cols(r, i):
-        return pl.ds(pl.multiple_of((r * own_heads + i) * wide, HS), wide)
-
-    def q_copy(i):
-        return remote(q_send.at[i], q_recv.at[i], q_ss.at[i], q_rs.at[i], across)
-
-    deep = 1024
-
-    def pieces(k):
-        return pl.ds(pl.multiple_of(k * deep, deep), deep)
-
-    def project(cols):
-        total[...] = jnp.zeros_like(total)
-
-        def step(k, carry):
-            total[...] += mm(nbuf[:, pieces(k)], wqkv[pieces(k), cols])
-            return carry
-
-        lax.fori_loop(0, width // deep, step, 0)
-
-    def project_there(i, carry):
-        project(head_cols(1 - row, i))
-        q_send[i] = total[...].astype(BF16)
-        q_copy(i).start()
+    project_piece(2)
+    gather_step(1, gbuf, 2)
+
+    def join(i, carry):
+        for j in range(3):
+            q_copy(i, j).wait_recv()
+        qkv[i] = (own_part[i] + q_recv[i].astype(F32)).astype(BF16)
         return carry
 
-    lax.fori_loop(0, own_heads, project_there, 0)
-    for d in range(2, chips):
-        gather_step(1, gbuf, d)
-        if d == 2:
-            def project_here(i, carry):
-                project(head_cols(row, i))
-                q_copy(i).wait_recv()
-                qkv[i] = (total[...] + q_recv[i].astype(F32)).astype(BF16)
-                return carry
-
-            lax.fori_loop(0, own_heads, project_here, 0)
+    lax.fori_loop(0, own_heads, join, 0)
 
     allowed = lax.broadcasted_iota(jnp.int32, (tokens, tokens), 1) <= lax.broadcasted_iota(
         jnp.int32, (tokens, tokens), 0
@@ -320,32 +344,45 @@
         return carry
 
     lax.fori_loop(0, own_heads, forward, 0)
-    gather_end(1, gbuf)
-    save_g = pltpu.make_async_copy(gbuf, g_out, out_sem.at[1])
-    save_g.start()
 
     load_out.wait()
     span = own_heads * HS
+    early = pl.ds(pl.multiple_of(jnp.where(low, 0, chip_rows), chip_rows), 3 * chip_rows)
+    parts = [(early, 3 * chip_rows), spans[2]]
 
     def out_rows(r):
         return pl.ds(pl.multiple_of(r * span, HS), span)
 
-    def context_part(r):
-        total[...] = jnp.zeros_like(total)
+    def context_part(r, here, count):
+        total[0:count] = jnp.zeros((count, span), F32)
 
         def step(k, carry):
-            total[...] += mm(gbuf[:, pieces(k)], wout[out_rows(r), pieces(k)], NT)
+            total[0:count] += mm(gbuf[here, pieces(k)], wout[out_rows(r), pieces(k)], NT)
             return carry
 
         lax.fori_loop(0, width // deep, step, 0)
 
-    context_part(1 - row)
-    dc_send[...] = total[...].astype(BF16)
-    dc_copy = remote(dc_send, dc_recv, dc_ss.at[0], dc_rs.at[0], across)
-    dc_copy.start()
-    context_part(row)
-    dc_copy.wait_recv()
-    dc = (total[...] + dc_recv[...].astype(F32)).astype(BF16)
+    dc_copies = []
+    for j in range(2):
+        here, count = parts[j]
+        if j == 0:
+            pair_wait(1, gbuf, near)
+            pair_wait(1, gbuf, near + 1)
+            pair_wait(1, gbuf, third)
+        else:
+            gather_step(1, gbuf, 3)
+            pair_wait(1, gbuf, last)
+            save_g = pltpu.make_async_copy(gbuf, g_out, out_sem.at[1])
+            save_g.start()
+        context_part(1 - row, here, count)
+        dc_send[here] = total[0:count].astype(BF16)
+        dc_copies.append(remote(dc_send.at[here], dc_recv.at[here], dc_ss.at[j], dc_rs.at[j], across))
+        dc_copies[j].start()
+        context_part(row, here, count)
+        own_part[0, here] = total[0:count]
+    for dc_copy in dc_copies:
+        dc_copy.wait_recv()
+    dc = (own_part[0] + dc_recv[...].astype(F32)).astype(BF16)
     for i in range(own_heads):
         dctx[i] = dc[:, i * HS:(i + 1) * HS]
 
@@ -370,6 +407,62 @@
         return carry
 
     lax.fori_loop(0, own_heads, backward, 0)
+    tile = 256
+
+    half_cols = own_heads * wide
+
+    def block_rows(b, which, cols):
+        return dqkv[pl.ds(pl.multiple_of((b * 2 + which) * rows, rows), rows), cols]
+
+    def stacked(b0, b1, cols):
+        order = [(b0, core), (b1, core), (b0, 1 - core), (b1, 1 - core)]
+        return jnp.concatenate([block_rows(b, which, cols) for b, which in order], axis=0)
+
+    def row_cols(r):
+        return pl.ds(pl.multiple_of(r * half_cols, HS), half_cols)
+
+    def tiled(body):
+        def step(t, carry):
+            body(pl.ds(pl.multiple_of(t * tile, tile), tile))
+            return carry
+
+        lax.fori_loop(0, width // tile, step, 0)
+
+    def keep(b0, b1, cols, out):
+        acc[b0, :, cols] = out[0:rows]
+        acc[b1, :, cols] = out[rows:2 * rows]
+        sib_send[b0, :, cols] = out[2 * rows:3 * rows].astype(BF16)
+        sib_send[b1, :, cols] = out[3 * rows:].astype(BF16)
+
+    def pair_copy(b):
+        return remote(sib_send.at[b], sib_recv.at[b], ps_ss.at[b], ps_rs.at[b], sibling)
+
+    def line_copy(b, up):
+        w = 0 if up else 1
+        return remote(z_send, z_recv.at[w], rs_ss.at[w], rs_rs.at[w], above if up else below)
+
+    def hop_far():
+        @pl.when(z == 0)
+        def _():
+            z_send[...] = acc[far].astype(BF16)
+            line_copy(far, True).start()
+
+        @pl.when(z == far)
+        def _():
+            z_send[...] = acc[0].astype(BF16)
+            line_copy(0, False).start()
+
+    def add_pair(b):
+        pair_copy(b).wait_recv()
+        acc[b] = acc[b] + sib_recv[b].astype(F32)
+
+    far = chips - 1
+    def own_share(cols):
+        out = mm(stacked(0, far, row_cols(row)), wqkv[cols, row_cols(row)], NT)
+        for k, b in enumerate((0, far, 1, 2)):
+            acc[b, :, cols] = out[k * rows:(k + 1) * rows]
+
+    tiled(own_share)
     for i in range(own_heads):
         there = dqkv.at[:, head_cols(1 - row, i)]
         remote(there, there, dq_ss.at[i], dq_rs.at[i], across).wait_recv()
@@ -383,58 +476,25 @@
         ctx_saves.append(pltpu.make_async_copy(ctx.at[h], to, ctx_sem.at[h]))
         ctx_saves[h].start()
 
-    tile = 256
-
-    def block_rows(b, which):
-        return dqkv[pl.ds(pl.multiple_of((b * 2 + which) * rows, rows), rows), :]
-
-    def partial_sums(b0, b1):
-        left = jnp.concatenate(
-            [block_rows(b0, core), block_rows(b1, core), block_rows(b0, 1 - core), block_rows(b1, 1 - core)],
-            axis=0,
-        )
-
-        def step(t, carry):
-            cols = pl.ds(pl.multiple_of(t * tile, tile), tile)
-            out = mm(left, wqkv[cols, :], NT)
-            acc[b0, :, cols] = out[0:rows]
-            acc[b1, :, cols] = out[rows:2 * rows]
-            sib_send[b0, :, cols] = out[2 * rows:3 * rows].astype(BF16)
-            sib_send[b1, :, cols] = out[3 * rows:].astype(BF16)
-            return carry
-
-        lax.fori_loop(0, width // tile, step, 0)
-        for b in (b0, b1):
-            pair_copy(b).start()
-
-    def pair_copy(b):
-        return remote(sib_send.at[b], sib_recv.at[b], ps_ss.at[b], ps_rs.at[b], sibling)
-
-    def line_copy(b, up):
-        w = 0 if up else 1
-        return remote(z_send, z_recv.at[w], rs_ss.at[w], rs_rs.at[w], above if up else below)
-
-    def hop_far():
-        @pl.when(z == 0)
-        def _():
-            z_send[...] = acc[far].astype(BF16)
-            line_copy(far, True).start()
-
-        @pl.when(z == far)
-        def _():
-            z_send[...] = acc[0].astype(BF16)
-            line_copy(0, False).start()
-
-    def add_pair(b):
-        pair_copy(b).wait_recv()
-        acc[b] = acc[b] + sib_recv[b].astype(F32)
-
-    far = chips - 1
-    partial_sums(0, far)
+    def other_share(cols):
+        out = mm(stacked(0, far, row_cols(1 - row)), wqkv[cols, row_cols(1 - row)], NT)
+        before = jnp.concatenate([acc[b, :, cols] for b in (0, far, 1, 2)], axis=0)
+        keep(0, far, cols, out + before)
+
+    tiled(other_share)
+    for b in (0, far):
+        pair_copy(b).start()
     add_pair(0)
     add_pair(far)
     hop_far()
-    partial_sums(1, 2)
+
+    def both_shares(cols):
+        every = slice(None)
+        keep(1, 2, cols, mm(stacked(1, 2, every), wqkv[cols, :], NT))
+
+    tiled(both_shares)
+    for b in (1, 2):
+        pair_copy(b).start()
     add_pair(1)
     add_pair(2)
 
@@ -467,10 +527,12 @@
     gather_drain(0, nbuf)
     gather_drain(1, gbuf)
     for i in range(own_heads):
-        q_copy(i).wait_send()
+        for j in range(3):
+            q_copy(i, j).wait_send()
         ctx_copy(i).wait_send()
         dq_copy(i).wait_send()
-    dc_copy.wait_send()
+    for dc_copy in dc_copies:
+        dc_copy.wait_send()
     for b in range(chips):
         pair_copy(b).wait_send()
 
@@ -547,6 +609,33 @@
     stats.wait_send()
     for k in range(1, peers):
         gg_copy(k, col).wait_send()
+
+
+def weight_gradient(left, right, tile, wide):
+    tokens, height = left.shape
+    columns = right.shape[1]
+
+    def kernel(left_ref, right_ref, out_ref):
+        turned = left_ref[...].T
+        for at in range(0, columns, wide):
+            out_ref[:, at:at + wide] = mm(turned, right_ref[:, at:at + wide]).astype(BF16)
+
+    return pl.pallas_call(
+        kernel,
+        grid=(height // tile,),
+        out_shape=jax.ShapeDtypeStruct((height, columns), BF16),
+        in_specs=[
+            pl.BlockSpec((tokens, tile), lambda i: (0, i)),
+            pl.BlockSpec((tokens, columns), lambda i: (0, 0)),
+        ],
+        out_specs=pl.BlockSpec((tile, columns), lambda i: (i, 0)),
+        compiler_params=pltpu.CompilerParams(vmem_limit_bytes=32 * 2**20),
+        cost_estimate=pl.CostEstimate(
+            flops=2 * tokens * height * columns,
+            bytes_accessed=2 * (tokens * (height + columns) + height * columns),
+            transcendentals=0,
+        ),
+    )(left, right)
 
 
 def pair_shards(layer_input, layer_norm_gain, w_qkv, w_out, out_grad):
@@ -602,10 +691,11 @@
             pltpu.VMEM((rows, width), BF16),
             pltpu.VMEM((2, rows, width), BF16),
             pltpu.VMEM((tokens, 3 * HS), F32),
+            pltpu.VMEM((own, tokens, 3 * HS), F32),
             dma((2,)), dma((10,)), dma((heads,)), dma((1,)), dma((1,)),
             dma((2, chips)), dma((2, chips)), dma((2, chips)), dma((2, chips)), dma((2, chips)),
-            dma((own,)), dma((own,)), dma((own,)), dma((own,)),
-            dma((1,)), dma((1,)), dma((own,)), dma((own,)),
+            dma((3, own)), dma((3, own)), dma((own,)), dma((own,)),
+            dma((2,)), dma((2,)), dma((own,)), dma((own,)),
             dma((chips,)), dma((chips,)), dma((2,)), dma((2,)),
         ],
         compiler_params=pltpu.CompilerParams(
@@ -620,12 +710,13 @@
     fall_first = [(2 * z + c, 2 * z - 2 + c) for z in range(half, chips) for c in both]
     got_up = lax.ppermute(onward, "col", rise_first)
     got_down = lax.ppermute(onward, "col", fall_first)
-    grad_wqkv = mm(normed, dqkv, TN).astype(BF16)
+    grad_wqkv = weight_gradient(normed, dqkv, 512, 3 * HS)
+    got_up, got_down, grad_wqkv = lax.optimization_barrier((got_up, got_down, grad_wqkv))
     next_up = (up + got_up.astype(F32)).astype(BF16)
     next_down = (down + got_down.astype(F32)).astype(BF16)
     from_below = lax.ppermute(next_up, "col", rise)
     from_above = lax.ppermute(next_down, "col", fall)
-    grad_wout = mm(context, grad, TN).astype(BF16)
+    grad_wout = weight_gradient(context, grad, HS, 4 * HS)
     dx, dgain = pl.pallas_call(
         norm_kernel,
         out_shape=[shape((rows, width), BF16), shape((1, width), F32)],

time: 165 us -> 161 us (0.976)
  matrix products: 20.9 us -> 0 us
  Pallas kernels: 130 us -> 145 us
  local copies, waits for them, and re-layouts: 1.39 us -> 4.54 us
    pallas_call x0 -> x2, Pallas kernels: none -> 21.6 us  [weight_gradient(): pl.pallas_call(kernel, grid=(height // tile,), out_shape=jax.ShapeDtypeSt...]
    dot_general x2 -> x0, matrix products: 20.9 us -> none  [mm(): return lax.dot_general(a, b, dims, preferred_element_type=F32)]
    pallas_call x1, Pallas kernels: 123 us -> 116 us  [pair_shards(): pl.pallas_call(functools.partial(block_kernel, chips), out_shape=[shape((...]
    unnamed x18 -> x22, local copies, waits for them, and re-layouts: 1.39 us -> 4.54 us
  transfers between devices with their start and end apart: 4 -> 4, of which waited for: 2 -> 2; matrix products, arithmetic and copies ran while one was open for 13% -> 0% of each run, Pallas kernels for 0% -> 14%
where the time goes in v3:
time: 161 us; the launch traced here: 160 us
  Pallas kernels  145 us (90%)
  starting transfers between devices  7.99 us (5%)
  local copies, waits for them, and re-layouts  4.54 us (3%)
    pallas_call x1, Pallas kernels, pair_shards(): pl.pallas_call(functools.partial(block_kernel, chips), out_shape=[shape((...  116 us
    pallas_call x2, Pallas kernels, weight_gradient(): pl.pallas_call(kernel, grid=(height // tile,), out_shape=jax.ShapeDtypeSt...  21.6 us
    pallas_call x1, Pallas kernels, pair_shards(): pl.pallas_call(norm_kernel, out_shape=[shape((rows, width), BF16), shape(...  7.22 us
    ppermute x1, starting transfers between devices, pair_shards(): from_below = lax.ppermute(next_up, 'col', rise)  4.57 us
    unnamed x22, local copies, waits for them, and re-layouts  4.54 us
  transfers between devices with their start and end apart: 4, of which 2 were waited for; matrix products, arithmetic and copies ran while one was open for 0% of the time, Pallas kernels for 14%

profile of v3, /device:TPU:0, one launch (start us, length us, event | category | flops | bytes accessed | tf_op | source)
XLA Modules:
  0.0 159.5 jit_solution(767891349445238662)
XLA Ops:
  0.6 115.8 %shard_map.84 = (bf16[256,6144]{1,0:T(8,128)(2,1)}, bf16[256,6144]{1,0:T(8,128)(2,1)}, bf16[256,768]{1,0:T(8,128)(2,1)}, bf16[256,2304]{1,0:T(8,128)(2,1)}, f32[...) custom-call(bf16[32,6144]{1,0:T(8,128)(2,1)} %x_ref.1, ...), custom_call_target="tpu_custom_call" | custom-call | tf_op jit(solution)/shard_map/pallas_call | solution.py:653
  116.5 1.3 collective-permute-start
  117.8 0.7 collective-permute-start.1
  118.5 0.0 copy-start.1
  118.5 1.9 %copy-done.1 = bf16[256,6144]{1,0:T(8,128)(2,1)S(1)} copy-done((bf16[256,6144]{1,0:T(8,128)(2,1)S(1)}, bf16[256,6144]{1,0:T(8,128)(2,1)}, u32[]{:S(2)}) %copy-start.1) | copy-done | bytes 3145752
  120.4 0.0 copy-start.2
  120.4 1.3 copy-done.2
  121.6 0.0 copy-start.9
  121.6 0.0 copy-start.8
  121.6 0.0 copy-start
  121.6 0.0 copy-start.5
  121.6 15.7 %shard_map.85 = bf16[6144,2304]{1,0:T(8,128)(2,1)} custom-call(bf16[256,6144]{1,0:T(8,128)(2,1)S(1)} %copy-done.1, bf16[256,2304]{1,0:T(8,128)(2,1)S(1)} %copy-done.2), custom_call_target="tpu_custom_call" | custom-call | flops 7247757312 | bytes 32636928 | tf_op jit(solution)/shard_map/pallas_call | solution.py:623
  137.3 0.0 copy-start.3
  137.3 0.0 copy-start.4
  137.3 0.0 copy-start.6
  137.3 0.0 copy-start.7
  137.3 0.0 collective-permute-done
  137.3 0.0 collective-permute-done.1
  137.3 0.0 copy-done.9
  137.4 0.1 add_convert_fusion
  137.4 1.4 collective-permute-start.3
  138.9 0.0 copy-done.8
  138.9 0.1 add_convert_fusion.1
  139.0 4.6 %collective-permute-start.2 = (bf16[32,6144]{1,0:T(8,128)(2,1)S(1)}, bf16[32,6144]{1,0:T(8,128)(2,1)S(1)}, u32[]{:S(2)}, u32[]{:S(2)}) collective-permute-start(bf16[32,6144]{1,0:T(8,128)(2,1)S(1)} %add_convert_fusion.1), channel_id=1, source_target_pairs={{0,4},{2,6},{4,8},{6,10},{8,12},{10,14},{1,5},{3,7},{5,9},{7,11},{... | collective-permute-start | bytes 1179656 | tf_op jit(solution)/shard_map/ppermute | solution.py:717
  143.5 0.0 copy-done
  143.5 0.0 copy-done.5
  143.5 5.9 %shard_map.87 = bf16[768,6144]{1,0:T(8,128)(2,1)} custom-call(bf16[256,768]{1,0:T(8,128)(2,1)S(1)} %copy-done.5, bf16[256,6144]{1,0:T(8,128)(2,1)S(1)} %copy-done), custom_call_target="tpu_custom_call" | custom-call | flops 2415919104 | bytes 12976128 | tf_op jit(solution)/shard_map/pallas_call | solution.py:623
  149.5 0.2 collective-permute-done.3.from_above
  149.6 1.3 collective-permute-done.2.from_below
  150.9 0.0 copy-done.3
  150.9 0.0 copy-done.4
  150.9 0.0 copy-done.6
  150.9 0.0 copy-done.7
  150.9 7.2 %shard_map.86 = (bf16[32,6144]{1,0:T(8,128)(2,1)S(1)}, f32[1,6144]{1,0:T(1,128)S(1)}) custom-call(f32[32,6144]{1,0:T(8,128)S(1)} %copy-done.4, bf16[32,6144]{1,0:T(8,128)(2,1)S(1)} %collective-permute-done.2.from_below, bf16[32,6144]{1,0:T(8,128)(2,1)S(1)} %collective-permute-done.3.from_above, f32[32,6144]{1,0:T(8,128)S(1)} %copy-done.3, ...), custom_call_target="tpu_custom_call" | custom-call | tf_op jit(solution)/shard_map/pallas_call | solution.py:720
  158.2 0.7 copy.11
  158.9 0.6 copy.12
Async XLA Ops:
  116.5 20.9 %collective-permute-start = (bf16[32,6144]{1,0:T(8,128)(2,1)}, bf16[32,6144]{1,0:T(8,128)(2,1)S(1)}, u32[]{:S(2)}, u32[]{:S(2)}) collective-permute-start(bf16[32,6144]{1,0:T(8,128)(2,1)} %get-tuple-element.21), channel_id=1, source_target_pairs={{0,4},{2,6},{4,8},{6,10},{1,5},{3,7},{5,9},{7,11},{16,20},{18,22},... | collective-permute-start | bytes 1179656 | tf_op jit(solution)/shard_map/ppermute | solution.py:711
  117.8 19.6 %collective-permute-start.1 = (bf16[32,6144]{1,0:T(8,128)(2,1)}, bf16[32,6144]{1,0:T(8,128)(2,1)S(1)}, u32[]{:S(2)}, u32[]{:S(2)}) collective-permute-start(bf16[32,6144]{1,0:T(8,128)(2,1)} %get-tuple-element.21), channel_id=1, source_target_pairs={{8,4},{10,6},{12,8},{14,10},{9,5},{11,7},{13,9},{15,11},{24,20},{2... | collective-permute-start | bytes 1179656 | tf_op jit(solution)/shard_map/ppermute | solution.py:712
  118.5 1.9 %copy-start.1 = (bf16[256,6144]{1,0:T(8,128)(2,1)S(1)}, bf16[256,6144]{1,0:T(8,128)(2,1)}, u32[]{:S(2)}) copy-start(bf16[256,6144]{1,0:T(8,128)(2,1)} %get-tuple-element.22.left_ref) | copy-start | bytes 9437188
  120.4 1.3 copy-start.2
  121.6 15.7 %copy-start.9 = (f32[32,6144]{1,0:T(8,128)S(1)}, f32[32,6144]{1,0:T(8,128)}, u32[]{:S(2)}) copy-start(f32[32,6144]{1,0:T(8,128)} %get-tuple-element.25) | copy-start | bytes 2359300
  121.6 17.2 %copy-start.8 = (f32[32,6144]{1,0:T(8,128)S(1)}, f32[32,6144]{1,0:T(8,128)}, u32[]{:S(2)}) copy-start(f32[32,6144]{1,0:T(8,128)} %get-tuple-element.20) | copy-start | bytes 2359300
  121.6 21.9 %copy-start = (bf16[256,6144]{1,0:T(8,128)(2,1)S(1)}, bf16[256,6144]{1,0:T(8,128)(2,1)}, u32[]{:S(2)}) copy-start(bf16[256,6144]{1,0:T(8,128)(2,1)} %get-tuple-element.33.right_ref) | copy-start | bytes 9437188
  121.6 21.9 %copy-start.5 = (bf16[256,768]{1,0:T(8,128)(2,1)S(1)}, bf16[256,768]{1,0:T(8,128)(2,1)}, u32[]{:S(2)}) copy-start(bf16[256,768]{1,0:T(8,128)(2,1)} %get-tuple-element.32.left_ref) | copy-start | bytes 1179652
  137.3 13.6 %copy-start.3 = (f32[32,6144]{1,0:T(8,128)S(1)}, f32[32,6144]{1,0:T(8,128)}, u32[]{:S(2)}) copy-start(f32[32,6144]{1,0:T(8,128)} %get-tuple-element.27.xhat_ref) | copy-start | bytes 2359300
  137.3 13.6 %copy-start.4 = (f32[32,6144]{1,0:T(8,128)S(1)}, f32[32,6144]{1,0:T(8,128)}, u32[]{:S(2)}) copy-start(f32[32,6144]{1,0:T(8,128)} %get-tuple-element.19.here_ref) | copy-start | bytes 2359300
  137.3 13.6 %copy-start.6 = (f32[6144]{0:T(1024)S(1)}, f32[6144]{0:T(1024)}, u32[]{:S(2)}) copy-start(f32[6144]{0:T(1024)} %param.6) | copy-start | bytes 73732
  137.3 13.6 %copy-start.7 = (f32[32,128]{1,0:T(8,128)S(1)}, f32[32,128]{1,0:T(8,128)}, u32[]{:S(2)}) copy-start(f32[32,128]{1,0:T(8,128)} %get-tuple-element.28.rstd_ref) | copy-start | bytes 49156
  137.4 12.2 %collective-permute-start.3 = (bf16[32,6144]{1,0:T(8,128)(2,1)S(1)}, bf16[32,6144]{1,0:T(8,128)(2,1)S(1)}, u32[]{:S(2)}, u32[]{:S(2)}) collective-permute-start(bf16[32,6144]{1,0:T(8,128)(2,1)S(1)} %add_convert_fusion), channel_id=1, source_target_pairs={{4,0},{6,2},{8,4},{10,6},{12,8},{14,10},{5,1},{7,3},{9,5},{11,7},{... | collective-permute-start | bytes 1179656 | tf_op jit(solution)/shard_map/ppermute | solution.py:718
  139.0 12.0 %collective-permute-start.2 = (bf16[32,6144]{1,0:T(8,128)(2,1)S(1)}, bf16[32,6144]{1,0:T(8,128)(2,1)S(1)}, u32[]{:S(2)}, u32[]{:S(2)}) collective-permute-start(bf16[32,6144]{1,0:T(8,128)(2,1)S(1)} %add_convert_fusion.1), channel_id=1, source_target_pairs={{0,4},{2,6},{4,8},{6,10},{8,12},{10,14},{1,5},{3,7},{5,9},{7,11},{... | collective-permute-start | bytes 1179656 | tf_op jit(solution)/shard_map/ppermute | solution.py:717

commit v4 on v3

--- a/solution.py
+++ b/solution.py
@@ -611,31 +611,36 @@
         gg_copy(k, col).wait_send()
 
 
-def weight_gradient(left, right, tile, wide):
+def weight_gradient(left, right, tile, wide, first, count, into=None):
     tokens, height = left.shape
     columns = right.shape[1]
 
-    def kernel(left_ref, right_ref, out_ref):
+    def kernel(left_ref, right_ref, *rest):
+        out_ref = rest[-1]
         turned = left_ref[...].T
         for at in range(0, columns, wide):
             out_ref[:, at:at + wide] = mm(turned, right_ref[:, at:at + wide]).astype(BF16)
 
+    specs = [
+        pl.BlockSpec((tokens, tile), lambda i: (0, i + first)),
+        pl.BlockSpec((tokens, columns), lambda i: (0, 0)),
+    ]
+    more = () if into is None else (into,)
+    rows = count * tile
     return pl.pallas_call(
         kernel,
-        grid=(height // tile,),
+        grid=(count,),
         out_shape=jax.ShapeDtypeStruct((height, columns), BF16),
-        in_specs=[
-            pl.BlockSpec((tokens, tile), lambda i: (0, i)),
-            pl.BlockSpec((tokens, columns), lambda i: (0, 0)),
-        ],
-        out_specs=pl.BlockSpec((tile, columns), lambda i: (i, 0)),
-        compiler_params=pltpu.CompilerParams(vmem_limit_bytes=32 * 2**20),
+        in_specs=specs + [pl.BlockSpec(memory_space=pl.ANY)] * len(more),
+        out_specs=pl.BlockSpec((tile, columns), lambda i: (i + first, 0)),
+        input_output_aliases={2: 0} if more else {},
+        compiler_params=pltpu.CompilerParams(vmem_limit_bytes=58 * 2**20),
         cost_estimate=pl.CostEstimate(
-            flops=2 * tokens * height * columns,
-            bytes_accessed=2 * (tokens * (height + columns) + height * columns),
+            flops=2 * tokens * rows * columns,
+            bytes_accessed=2 * (tokens * (rows + columns) + rows * columns),
             transcendentals=0,
         ),
-    )(left, right)
+    )(left, right, *more)
 
 
 def pair_shards(layer_input, layer_norm_gain, w_qkv, w_out, out_grad):
@@ -710,13 +715,17 @@
     fall_first = [(2 * z + c, 2 * z - 2 + c) for z in range(half, chips) for c in both]
     got_up = lax.ppermute(onward, "col", rise_first)
     got_down = lax.ppermute(onward, "col", fall_first)
-    grad_wqkv = weight_gradient(normed, dqkv, 512, 3 * HS)
+    tile = 512
+    tiles = width // tile
+    early = 2 * tiles // 3
+    grad_wqkv = weight_gradient(normed, dqkv, tile, 3 * HS, 0, early)
     got_up, got_down, grad_wqkv = lax.optimization_barrier((got_up, got_down, grad_wqkv))
     next_up = (up + got_up.astype(F32)).astype(BF16)
     next_down = (down + got_down.astype(F32)).astype(BF16)
     from_below = lax.ppermute(next_up, "col", rise)
     from_above = lax.ppermute(next_down, "col", fall)
-    grad_wout = weight_gradient(context, grad, HS, 4 * HS)
+    grad_wqkv = weight_gradient(normed, dqkv, tile, 3 * HS, early, tiles - early, grad_wqkv)
+    grad_wout = mm(context, grad, TN).astype(BF16)
     dx, dgain = pl.pallas_call(
         norm_kernel,
         out_shape=[shape((rows, width), BF16), shape((1, width), F32)],

time: 161 us -> 159 us (0.988)
  matrix products: 0 us -> 5.18 us
  starting transfers between devices: 7.99 us -> 4.58 us
  local copies, waits for them, and re-layouts: 4.54 us -> 1.39 us
    dot_general x0 -> x1, matrix products: none -> 5.18 us  [mm(): return lax.dot_general(a, b, dims, preferred_element_type=F32)]
    ppermute x1, starting transfers between devices: 4.57 us -> 1.3 us  [pair_shards(): from_below = lax.ppermute(next_up, 'col', rise)]
    unnamed x22 -> x18, local copies, waits for them, and re-layouts: 4.54 us -> 1.39 us
    pallas_call x1, Pallas kernels: 7.22 us -> 9.71 us  [pair_shards(): pl.pallas_call(norm_kernel, out_shape=[shape((rows, width), BF16), shape(...]
    pallas_call x2, Pallas kernels: 21.6 us -> 19.8 us  [weight_gradient(): pl.pallas_call(kernel, grid=(count,), out_shape=jax.ShapeDtypeStruct((hei...]
  transfers between devices with their start and end apart: 4 -> 4, of which waited for: 2 -> 0; matrix products, arithmetic and copies ran while one was open for 0% -> 4% of each run, Pallas kernels for 14% -> 12%
where the time goes in v4:
time: 159 us
  Pallas kernels  145 us (91%)
  matrix products  5.18 us (3%)
  starting transfers between devices  4.58 us (3%)
  other arithmetic  1.67 us (1%)
    pallas_call x1, Pallas kernels, pair_shards(): pl.pallas_call(functools.partial(block_kernel, chips), out_shape=[shape((...  116 us
    pallas_call x2, Pallas kernels, weight_gradient(): pl.pallas_call(kernel, grid=(count,), out_shape=jax.ShapeDtypeStruct((hei...  19.8 us
    pallas_call x1, Pallas kernels, pair_shards(): pl.pallas_call(norm_kernel, out_shape=[shape((rows, width), BF16), shape(...  9.71 us
    dot_general x1, matrix products, mm(): return lax.dot_general(a, b, dims, preferred_element_type=F32)  5.18 us
  transfers between devices with their start and end apart: 4, of which 0 were waited for; matrix products, arithmetic and copies ran while one was open for 4% of the time, Pallas kernels for 12%

profile of v4, /device:TPU:0, one launch (start us, length us, event | category | flops | bytes accessed | tf_op | source)
XLA Modules:
  0.0 158.9 jit_solution(2664795695734433563)
XLA Ops:
  0.6 115.8 %shard_map.84 = (bf16[256,6144]{1,0:T(8,128)(2,1)}, bf16[256,6144]{1,0:T(8,128)(2,1)}, bf16[256,768]{1,0:T(8,128)(2,1)}, bf16[256,2304]{1,0:T(8,128)(2,1)}, f32[...) custom-call(bf16[32,6144]{1,0:T(8,128)(2,1)} %x_ref.1, ...), custom_call_target="tpu_custom_call" | custom-call | tf_op jit(solution)/shard_map/pallas_call | solution.py:658
  116.4 1.3 collective-permute-start
  117.8 0.7 collective-permute-start.1
  118.5 0.0 copy-start.6
  118.5 0.0 copy-start.5
  118.5 0.0 copy-start.4
  118.5 0.0 copy-start.7
  118.5 12.3 %shard_map.85.rest_0_ = bf16[6144,2304]{1,0:T(8,128)(2,1)} custom-call(bf16[256,6144]{1,0:T(8,128)(2,1)} %get-tuple-element.22.left_ref, bf16[256,2304]{1,0:T(8,128)(2,1)} %get-tuple-element.23.right_ref), custom_call_target="tpu_custom_call" | custom-call | flops 4831838208 | bytes 22151168 | tf_op jit(solution)/shard_map/pallas_call | solution.py:630
  130.8 0.0 collective-permute-done
  130.8 0.0 collective-permute-done.1
  130.8 0.0 copy-done.6
  130.8 0.8 add_convert_fusion.1
  131.6 1.3 collective-permute-start.2
  133.0 0.0 copy-done.5
  133.0 0.9 add_convert_fusion
  133.8 1.3 collective-permute-start.3
  135.1 0.0 copy-done.4
  135.1 0.0 copy-done.7
  135.1 5.2 %convolution_convert_fusion = bf16[768,6144]{1,0:T(8,128)(2,1)} fusion(bf16[256,768]{1,0:T(8,128)(2,1)S(1)} %copy-done.7, bf16[256,6144]{1,0:T(8,128)(2,1)S(1)} %copy-done.4), kind=kOutput, calls=%fused_computation | convolution fusion | flops 2420637696 | bytes 12976128 | tf_op jit(solution)/shard_map/dot_general | solution.py:122
  140.3 0.0 copy-start
  140.3 0.0 copy-start.1
  140.3 0.0 copy-start.2
  140.3 0.0 copy-start.3
  140.3 7.5 %shard_map.87 = bf16[6144,2304]{1,0:T(8,128)(2,1)} custom-call(bf16[256,6144]{1,0:T(8,128)(2,1)} %get-tuple-element.22.left_ref, bf16[256,2304]{1,0:T(8,128)(2,1)} %get-tuple-element.23.right_ref, bf16[6144,2304]{1,0:T(8,128)(2,1)} %shard_map.85.rest_0_), custom_call_target="tpu_custom_call", output_to_operand_aliasing={{}: (2, {})} | custom-call | flops 2415919104 | bytes 11665408 | tf_op jit(solution)/shard_map/pallas_call | solution.py:630
  147.8 0.0 collective-permute-done.2.from_below
  147.8 0.0 collective-permute-done.3.from_above
  147.8 0.0 copy-done
  147.8 0.0 copy-done.1
  147.8 0.0 copy-done.2
  147.8 0.0 copy-done.3
  147.8 9.7 %shard_map.86 = (bf16[32,6144]{1,0:T(8,128)(2,1)S(1)}, f32[1,6144]{1,0:T(1,128)S(1)}) custom-call(f32[32,6144]{1,0:T(8,128)S(1)} %copy-done.1, bf16[32,6144]{1,0:T(8,128)(2,1)S(1)} %collective-permute-done.2.from_below, bf16[32,6144]{1,0:T(8,128)(2,1)S(1)} %collective-permute-done.3.from_above, f32[32,6144]{1,0:T(8,128)S(1)} %copy-done, ...), custom_call_target="tpu_custom_call" | custom-call | tf_op jit(solution)/shard_map/pallas_call | solution.py:729
  157.5 0.7 copy.13
  158.3 0.6 copy.14
Async XLA Ops:
  116.4 14.4 %collective-permute-start = (bf16[32,6144]{1,0:T(8,128)(2,1)}, bf16[32,6144]{1,0:T(8,128)(2,1)S(1)}, u32[]{:S(2)}, u32[]{:S(2)}) collective-permute-start(bf16[32,6144]{1,0:T(8,128)(2,1)} %get-tuple-element.21), channel_id=1, source_target_pairs={{0,4},{2,6},{4,8},{6,10},{1,5},{3,7},{5,9},{7,11},{16,20},{18,22},... | collective-permute-start | bytes 1179656 | tf_op jit(solution)/shard_map/ppermute | solution.py:716
  117.8 13.1 %collective-permute-start.1 = (bf16[32,6144]{1,0:T(8,128)(2,1)}, bf16[32,6144]{1,0:T(8,128)(2,1)S(1)}, u32[]{:S(2)}, u32[]{:S(2)}) collective-permute-start(bf16[32,6144]{1,0:T(8,128)(2,1)} %get-tuple-element.21), channel_id=1, source_target_pairs={{8,4},{10,6},{12,8},{14,10},{9,5},{11,7},{13,9},{15,11},{24,20},{2... | collective-permute-start | bytes 1179656 | tf_op jit(solution)/shard_map/ppermute | solution.py:717
  118.5 12.4 %copy-start.6 = (f32[32,6144]{1,0:T(8,128)S(1)}, f32[32,6144]{1,0:T(8,128)}, u32[]{:S(2)}) copy-start(f32[32,6144]{1,0:T(8,128)} %get-tuple-element.20) | copy-start | bytes 2359300
  118.5 14.5 %copy-start.5 = (f32[32,6144]{1,0:T(8,128)S(1)}, f32[32,6144]{1,0:T(8,128)}, u32[]{:S(2)}) copy-start(f32[32,6144]{1,0:T(8,128)} %get-tuple-element.25) | copy-start | bytes 2359300
  118.5 16.6 %copy-start.4 = (bf16[256,6144]{1,0:T(8,128)(2,1)S(1)}, bf16[256,6144]{1,0:T(8,128)(2,1)}, u32[]{:S(2)}) copy-start(bf16[256,6144]{1,0:T(8,128)(2,1)} %get-tuple-element.33) | copy-start | bytes 9437188
  118.5 16.6 %copy-start.7 = (bf16[256,768]{1,0:T(8,128)(2,1)S(1)}, bf16[256,768]{1,0:T(8,128)(2,1)}, u32[]{:S(2)}) copy-start(bf16[256,768]{1,0:T(8,128)(2,1)} %get-tuple-element.32) | copy-start | bytes 1179652
  131.6 16.1 %collective-permute-start.2 = (bf16[32,6144]{1,0:T(8,128)(2,1)}, bf16[32,6144]{1,0:T(8,128)(2,1)S(1)}, u32[]{:S(2)}, u32[]{:S(2)}) collective-permute-start(bf16[32,6144]{1,0:T(8,128)(2,1)} %add_convert_fusion.1), channel_id=1, source_target_pairs={{0,4},{2,6},{4,8},{6,10},{8,12},{10,14},{1,5},{3,7},{5,9},{7,11},{... | collective-permute-start | bytes 1179656 | tf_op jit(solution)/shard_map/ppermute | solution.py:725
  133.8 14.0 %collective-permute-start.3 = (bf16[32,6144]{1,0:T(8,128)(2,1)}, bf16[32,6144]{1,0:T(8,128)(2,1)S(1)}, u32[]{:S(2)}, u32[]{:S(2)}) collective-permute-start(bf16[32,6144]{1,0:T(8,128)(2,1)} %add_convert_fusion), channel_id=1, source_target_pairs={{4,0},{6,2},{8,4},{10,6},{12,8},{14,10},{5,1},{7,3},{9,5},{11,7},{... | collective-permute-start | bytes 1179656 | tf_op jit(solution)/shard_map/ppermute | solution.py:726
  140.3 7.5 %copy-start = (f32[32,6144]{1,0:T(8,128)S(1)}, f32[32,6144]{1,0:T(8,128)}, u32[]{:S(2)}) copy-start(f32[32,6144]{1,0:T(8,128)} %get-tuple-element.27.xhat_ref) | copy-start | bytes 2359300
  140.3 7.5 %copy-start.1 = (f32[32,6144]{1,0:T(8,128)S(1)}, f32[32,6144]{1,0:T(8,128)}, u32[]{:S(2)}) copy-start(f32[32,6144]{1,0:T(8,128)} %get-tuple-element.19.here_ref) | copy-start | bytes 2359300
  140.3 7.5 %copy-start.2 = (f32[6144]{0:T(1024)S(1)}, f32[6144]{0:T(1024)}, u32[]{:S(2)}) copy-start(f32[6144]{0:T(1024)} %param.6) | copy-start | bytes 73732
  140.3 7.5 %copy-start.3 = (f32[32,128]{1,0:T(8,128)S(1)}, f32[32,128]{1,0:T(8,128)}, u32[]{:S(2)}) copy-start(f32[32,128]{1,0:T(8,128)} %get-tuple-element.28.rstd_ref) | copy-start | bytes 49156
